TPU v7x, 512 devices: a whole 4x4x16 slice. The times are simulated.
512 devices in a mesh: dp: 8 (over y, core), frame: 64 (over z, x).
Axes of the slice: x: 4, y: 4, z: 16, core: 2. Of those that a mesh axis runs over, the one named last changes fastest.
Arguments:
- frame_features: bfloat16 [8, 2048, 8, 1536], P('dp', 'frame'), may hold values from -6 to 6
- frame_owner: int32 [8, 2048, 1], P('dp', 'frame'), may hold values from 0 to 63; in each aligned block of 32 rows (0 to 31, 32 to 63, ..., all dimensions but the last counted through in order) no two rows name the same one
- latents: float32 [64, 1536], replicated, may hold values from -10 to 10
- latent_gain: float32 [1536], replicated, may hold values from 0.25 to 1.75
- media_gain: float32 [1536], replicated, may hold values from 0.25 to 1.75
- query_proj: bfloat16 [1536, 512], P(('dp', 'frame')), may hold values from -0.3 to 0.3
- keyval_proj: bfloat16 [1536, 1024], P(('dp', 'frame')), may hold values from -0.3 to 0.3
- grad_output: bfloat16 [8, 64, 64, 512], P('dp', 'frame'), may hold values from -6 to 6
Outputs:
- attended: bfloat16 [8, 64, 64, 512], P('dp', 'frame')
- latent_grad: float32 [64, 1536], replicated
- latent_gain_grad: float32 [1536], replicated
- media_gain_grad: float32 [1536], replicated
Inputs may be any that keep to these rules, and one draw needn't show every extreme that they name: `frame_owner`: of the 32 frames of one device, at most 1 belong to one sample, and in every draw some device sends exactly 1 frames to some sample.
All inputs are finite; a program needn't handle non-finite values.
Results may differ from a plain program's by a relative error of at most 0.012.
The roundings to bfloat16 on the way count: a program that leaves them out, or rounds other values in their place, can miss the bound.
Values may be sent and summed in bfloat16 or wider, within the bound.
A program may use at most 64 MiB of HBM per device.

v0:
```python
import jax
import jax.numpy as jnp
from jax import lax
from jax.sharding import PartitionSpec as P

HEADS = 8


def norm_rows(values):
    center = values - jnp.mean(values, -1, keepdims=True)
    inverse = lax.rsqrt(jnp.mean(center * center, -1, keepdims=True) + 1e-05)
    return (center * inverse, inverse)


def precise_times(left, weight):
    upper = left.astype(jnp.bfloat16)
    lower = (left - upper.astype(jnp.float32)).astype(jnp.bfloat16)
    dims = (((1,), (1,)), ((), ()))
    first = lax.dot_general(upper, weight, dims, preferred_element_type=jnp.float32)
    return first + lax.dot_general(lower, weight, dims, preferred_element_type=jnp.float32)


def attend(query, key_rows, live_keys, gradient, head_count):
    inner_width = query.shape[1]
    head_size = inner_width // head_count
    query_heads = query.reshape(-1, head_count, head_size)
    key_heads = key_rows[:, :inner_width].reshape(-1, head_count, head_size)
    value_heads = key_rows[:, inner_width:].reshape(-1, head_count, head_size)
    scores = jnp.einsum("qhd,khd->hqk", query_heads, key_heads, preferred_element_type=jnp.float32)
    scores = jnp.where(live_keys[None, None, :], scores, -jnp.inf)
    weights = jax.nn.softmax(scores, axis=-1)
    weights_low = weights.astype(jnp.bfloat16)
    attended = jnp.einsum(
        "hqk,khd->qhd", weights_low, value_heads, preferred_element_type=jnp.float32
    )
    attended = attended.reshape(-1, inner_width).astype(jnp.bfloat16)
    grad_heads = gradient.reshape(-1, head_count, head_size)
    grad_weights = jnp.einsum(
        "qhd,khd->hqk", grad_heads, value_heads, preferred_element_type=jnp.float32
    )
    grad_scores = weights * (grad_weights - jnp.sum(weights * grad_weights, -1, keepdims=True))
    grad_scores = grad_scores.astype(jnp.bfloat16)
    grad_query = jnp.einsum(
        "hqk,khd->qhd", grad_scores, key_heads, preferred_element_type=jnp.float32
    )
    grad_key = jnp.einsum(
        "hqk,qhd->khd", grad_scores, query_heads, preferred_element_type=jnp.float32
    )
    grad_value = jnp.einsum(
        "hqk,qhd->khd", weights_low, grad_heads, preferred_element_type=jnp.float32
    )
    grad_keyval = jnp.concatenate(
        [grad_key.reshape(-1, inner_width), grad_value.reshape(-1, inner_width)], axis=1
    )
    return (attended, grad_query.reshape(-1, inner_width), grad_keyval)


def body(
    frame_features,
    frame_owner,
    latents,
    latent_gain,
    media_gain,
    query_proj,
    keyval_proj,
    grad_output,
):
    owners = lax.axis_size("frame")
    inner_width = query_proj.shape[1]
    score_scale = (inner_width // HEADS) ** (-0.5)
    full_keyval = lax.all_gather(keyval_proj, ("dp", "frame"), axis=0, tiled=True)
    latent_hat, latent_inv = norm_rows(latents)
    latent_norm = (latent_hat * latent_gain).astype(jnp.bfloat16)
    full_query = lax.all_gather(query_proj, ("dp", "frame"), axis=0, tiled=True)
    query_raw = jnp.dot(latent_norm, full_query, preferred_element_type=jnp.float32)
    query = (query_raw * score_scale).astype(jnp.bfloat16)
    latent_keyval = jnp.dot(latent_norm, full_keyval, preferred_element_type=jnp.float32).astype(
        jnp.bfloat16
    )
    frames = frame_features[0]
    frame_count, frame_tokens, width = frames.shape
    slot_cap = max(1, -(-frame_count // owners))
    media_hat, _ = norm_rows(frames.astype(jnp.float32))
    media_norm = (media_hat * media_gain).astype(jnp.bfloat16)
    route = frame_owner[0, :, 0]
    by_owner = (route[None, :] == jnp.arange(owners, dtype=jnp.int32)[:, None]).astype(jnp.int32)
    rank_within = jnp.sum(by_owner * jnp.cumsum(by_owner, axis=1), axis=0) - 1
    slot_index = route * slot_cap + rank_within
    selected = slot_index[None, :] == jnp.arange(owners * slot_cap, dtype=jnp.int32)[:, None]
    slot_live = jnp.sum(selected.astype(jnp.int32), axis=1).reshape(owners, slot_cap)
    selector = selected.astype(jnp.bfloat16)
    packed = jnp.dot(
        selector, media_norm.reshape(frame_count, -1), preferred_element_type=jnp.float32
    )
    received = lax.all_to_all(
        packed.astype(jnp.bfloat16).reshape(owners, slot_cap, frame_tokens, -1),
        "frame",
        split_axis=0,
        concat_axis=0,
        tiled=True,
    )
    live_slots = lax.all_to_all(slot_live, "frame", split_axis=0, concat_axis=0, tiled=True)
    media_keyval = jnp.dot(
        received.reshape(-1, width), full_keyval, preferred_element_type=jnp.float32
    ).astype(jnp.bfloat16)
    media_rows = media_keyval.shape[0]
    key_rows = jnp.concatenate([media_keyval, latent_keyval], axis=0)
    live_keys = jnp.concatenate(
        [jnp.repeat(live_slots.reshape(-1) > 0, frame_tokens), jnp.ones((latents.shape[0],), bool)]
    )
    attended, grad_query, grad_keyval = attend(query, key_rows, live_keys, grad_output[0, 0], HEADS)
    grad_media = grad_keyval[:media_rows].astype(jnp.bfloat16)
    grad_slots = (
        lax.dot_general(
            grad_media, full_keyval, (((1,), (1,)), ((), ())), preferred_element_type=jnp.float32
        )
        .astype(jnp.bfloat16)
        .reshape(owners, slot_cap, frame_tokens, width)
    )
    returned = lax.all_to_all(grad_slots, "frame", split_axis=0, concat_axis=0, tiled=True)
    flat = returned.reshape(owners * slot_cap, -1)
    frame_rows = lax.dot_general(
        selector, flat, (((0,), (0,)), ((), ())), preferred_element_type=jnp.float32
    )
    grad_norm = frame_rows.astype(jnp.bfloat16).reshape(frame_count, frame_tokens, -1)
    media_term = jnp.sum(grad_norm.astype(jnp.float32) * media_hat, axis=(0, 1))
    query_sum, latent_sum, media_gain_grad = lax.psum(
        (grad_query * score_scale, grad_keyval[media_rows:], media_term), ("dp", "frame")
    )
    from_keyval = precise_times(latent_sum, full_keyval)
    from_query = precise_times(query_sum, full_query)
    grad_latent_norm = from_query + from_keyval
    latent_gain_grad = jnp.sum(grad_latent_norm * latent_hat, axis=0)
    grad_hat = grad_latent_norm * latent_gain
    latent_grad = latent_inv * (
        grad_hat
        - jnp.mean(grad_hat, -1, keepdims=True)
        - latent_hat * jnp.mean(grad_hat * latent_hat, -1, keepdims=True)
    )
    return (attended[None, None], latent_grad, latent_gain_grad, media_gain_grad)


def solution(mesh):
    placed = (
        P("dp", "frame", None, None),
        P("dp", "frame", None),
        P(),
        P(),
        P(),
        P(("dp", "frame"), None),
        P(("dp", "frame"), None),
        P("dp", "frame", None, None),
    )
    return jax.shard_map(
        body,
        mesh=mesh,
        in_specs=placed,
        out_specs=(P("dp", "frame", None, None), P(), P(), P()),
        check_vma=False,
    )
```

profile of v0, /device:TPU:1, one launch (start us, length us, event | category | flops | bytes accessed | tf_op | source)
XLA Modules:
  0.0 1077.9 jit_solution(18385940829629466917)
XLA Ops:
  7.2 0.7 all-gather.7.cloned.1.call-update
  7.9 0.7 fusion.30
  8.8 0.7 select_reduce_fusion
  9.5 0.7 add_add_fusion
  10.2 0.7 copy.50
  10.9 19.1 %all-to-all-start.1 = ((s32[64,1,1]{2,1,0:T(1,128)}), s32[64,1,1]{2,1,0:T(1,128)S(1)}, u32[]{:S(2)}, u32[]{:S(2)}) async-start(s32[64,1,1]{2,1,0:T(1,128)} %copy.50), calls=%async_computation.1 | async-start | bytes 65536 | tf_op jit(solution)/shard_map/all_to_all | solution.py:102
  30.1 0.7 all-gather.5.cloned.1.call-update
  30.8 1.3 convert_reduce_fusion
  32.7 0.9 copy.62
  34.1 0.9 copy.61
  35.4 0.7 convolution_convert_fusion
  36.2 1.7 copy.63
  37.9 5.6 all-to-all-done.1
  43.4 9.5 all-to-all-start
  52.9 0.8 copy.59
  54.1 1.2 compare_reduce_fusion
  55.5 0.6 concatenate.10
  56.1 170.7 %all-gather.7.cloned.1.call-done = bf16[512,3,512]{2,1,0:T(4,128)(2,1)} async-done(((bf16[1,3,512]{2,1,0:T(4,128)(2,1)}), bf16[512,3,512]{2,1,0:T(4,128)(2,1)}) %all-gather.7.cloned.1.call-update) | async-done | bytes 1572880 | tf_op jit(solution)/shard_map/all_gather | solution.py:74
  226.8 3.9 reshape.135
  230.7 0.4 fusion.16
  231.1 0.8 copy.58
  231.9 192.9 %all-gather.5.cloned.1.call-done = bf16[512,3,1024]{2,1,0:T(4,128)(2,1)} async-done(((bf16[1,3,1024]{2,1,0:T(4,128)(2,1)}), bf16[512,3,1024]{2,1,0:T(4,128)(2,1)}) %all-gather.5.cloned.1.call-update) | async-done | bytes 3145744 | tf_op jit(solution)/shard_map/all_gather | solution.py:71
  424.9 7.5 reshape.133
  432.4 1.4 convolution_convert_fusion.4
  433.7 3.2 fusion.11
  437.0 1.1 pad_maximum_fusion.1
  438.1 2.1 copy.49
  440.2 2.1 copy.51
  442.4 2.7 fusion.36
  445.1 3.0 fusion.21
  448.1 2.1 multiply_reduce_fusion
  450.5 0.8 copy-done.10
  451.6 1.1 copy-done.12
  452.8 3.0 fusion.3
  455.8 9.9 all-to-all-start.2
  466.0 2.0 fusion.20
  468.0 1.1 convolution_multiply_fusion
  469.1 2.8 convolution_convert_fusion.3
  471.9 1.6 copy.57
  473.5 481.4 %all-reduce.4.cloned.1.call-done = (f32[64,512]{0,1:T(8,128)}, f32[64,1024]{0,1:T(8,128)}) async-done(((f32[64,512]{0,1:T(8,128)}, f32[64,1024]{0,1:T(8,128)}), (f32[64,512]{0,1:T(8,128)}, f32[64,1024]{0,1:T(8,128)})) %all-reduce.4.cloned.1.call-update) | async-done | bytes 393232 | tf_op jit(solution)/shard_map/psum | solution.py:127
  954.9 2.2 fusion.28
  957.1 0.6 convolution_add_fusion.1
  958.1 1.1 fusion.25
  959.2 1.8 multiply_reduce_fusion.1
  961.0 0.9 subtract_multiply_fusion.1
  961.9 2.1 copy.64
  964.3 2.2 fusion.15
  966.5 104.9 %psum.23 = f32[1536]{0:T(1024)} all-reduce(f32[1536]{0:T(1024)S(1)} %reduce_sum.128), channel_id=1, replica_groups=mesh['dp'=8,'frame'=64] {'dp','frame'}, use_global_device_ids=true, to_apply=%region_17.18 | all-reduce | flops 1536 | bytes 12288 | tf_op jit(solution)/shard_map/psum | solution.py:127
  (77 shorter events, 4.0 us)
Async XLA Ops:
  7.2 25.0 %copy-start.8 = (bf16[1,32,8,1536]{3,2,1,0:T(8,128)(2,1)S(1)}, bf16[1,32,8,1536]{3,2,1,0:T(8,128)(2,1)}, u32[]{:S(2)}) copy-start(bf16[1,32,8,1536]{3,2,1,0:T(8,128)(2,1)} %param.8) | copy-start | bytes 2359300
  7.2 25.3 %copy-start.23 = (f32[1536]{0:T(1024)S(1)}, f32[1536]{0:T(1024)}, u32[]{:S(2)}) copy-start(f32[1536]{0:T(1024)} %param.12) | copy-start | bytes 18436
  7.2 219.6 %all-gather.7.cloned.1.call-start = ((), (), s32[]{:S(2)}) async-start(), calls=%async_computation.4 | async-start | bytes 2101248 | tf_op jit(solution)/shard_map/all_gather | solution.py:74
  10.1 24.9 %copy-start.24 = (s32[32]{0:T(128)}, s32[32]{0:T(128)S(1)}, u32[]{:S(2)}) copy-start(s32[32]{0:T(128)S(1)} %add_add_fusion) | copy-start | bytes 388
  10.9 32.5 %all-to-all-start.1 = ((s32[64,1,1]{2,1,0:T(1,128)}), s32[64,1,1]{2,1,0:T(1,128)S(1)}, u32[]{:S(2)}, u32[]{:S(2)}) async-start(s32[64,1,1]{2,1,0:T(1,128)} %copy.50), calls=%async_computation.1 | async-start | bytes 65536 | tf_op jit(solution)/shard_map/all_to_all | solution.py:102
  30.0 394.8 %all-gather.5.cloned.1.call-start = ((), (), s32[]{:S(2)}) async-start(), calls=%async_computation.3 | async-start | bytes 4202496 | tf_op jit(solution)/shard_map/all_gather | solution.py:71
  33.6 1.4 copy-start.3
  33.9 1.5 copy-start.5
  35.0 1.1 copy-start.7
  43.4 9.5 copy-start.20
  43.4 10.3 copy-start.2
  43.4 390.3 %all-to-all-start = ((bf16[64,1,8,1536]{3,2,1,0:T(8,128)(2,1)}), bf16[64,1,8,1536]{3,2,1,0:T(8,128)(2,1)}, u32[]{:S(2)}, u32[]{:S(2)}) async-start(bf16[64,1,8,1536]{3,2,1,0:T(8,128)(2,1)} %bitcast.2), calls=%async_computation | async-start | bytes 3145728 | tf_op jit(solution)/shard_map/all_to_all | solution.py:95
  54.1 378.3 %copy-start.21 = (f32[64]{0:T(128)}, f32[64]{0:T(128)S(1)}, u32[]{:S(2)}) copy-start(f32[64]{0:T(128)S(1)} %add_rsqrt_fusion.1) | copy-start | bytes 772
  56.1 174.6 %copy-start.19 = (f32[1536]{0:T(1024)S(1)}, f32[1536]{0:T(1024)}, u32[]{:S(2)}) copy-start(f32[1536]{0:T(1024)} %param.11) | copy-start | bytes 18436
  230.7 1.2 copy-start
  433.7 3.2 copy-start.18
  448.1 2.1 copy-start.13
  450.2 1.1 copy-start.16
  450.5 0.8 copy-start.10
  451.3 1.5 copy-start.15
  451.6 1.1 copy-start.12
  455.8 506.1 %all-to-all-start.2 = ((bf16[64,1,8,1536]{3,2,1,0:T(8,128)(2,1)}), bf16[64,1,8,1536]{3,2,1,0:T(8,128)(2,1)}, u32[]{:S(2)}, u32[]{:S(2)}) async-start(bf16[64,1,8,1536]{3,2,1,0:T(8,128)(2,1)} %fusion.3), calls=%async_computation.2 | async-start | bytes 3145728 | tf_op jit(solution)/shard_map/all_to_all | solution.py:120
  465.7 489.2 %all-reduce.4.cloned.1.call-start = ((), (), s32[]{:S(2)}) async-start(), calls=%async_computation.5 | async-start | bytes 1572864 | tf_op jit(solution)/shard_map/psum | solution.py:127
  466.0 2.0 copy-start.9
  466.0 2.0 copy-start.11
  954.9 2.2 copy-start.1
  954.9 2.2 copy-start.17
  957.1 1.0 copy-start.14
  958.1 1.1 copy-start.22
  961.9 2.1 copy-start.4
  961.9 2.4 copy-start.6
  961.9 2.4 copy-start.25
Sparse Core Ops, SparseCore 0:
  12.6 214.1 all-gather.6
  231.3 193.4 all-gather.4
  472.6 482.2 all-reduce.3
where the time goes:
time: 1080 us
  waiting for transfers between devices  852 us (79%)
  blocking collectives  105 us (10%)
  starting transfers between devices  38.8 us (4%)
  local copies, waits for them, and re-layouts  29.7 us (3%)
  matrix products  28.6 us (3%)
  between operations  14.1 us (1%)
    psum x1, waiting for transfers between devices, body(): lax.psum((grad_query * score_scale, grad_keyval[media_rows:], media_term)...  481 us
    all_gather x1, waiting for transfers between devices, body(): lax.all_gather(keyval_proj, ('dp', 'frame'), axis=0, tiled=True)  193 us
    all_gather x1, waiting for transfers between devices, body(): full_query = lax.all_gather(query_proj, ('dp', 'frame'), axis=0, tiled=True)  171 us
    psum x1, blocking collectives, body(): lax.psum((grad_query * score_scale, grad_keyval[media_rows:], media_term)...  105 us
    unnamed x60, local copies, waits for them, and re-layouts  22.1 us
  transfers between devices with their start and end apart: 6, of which 4 were waited for; matrix products, arithmetic and copies ran while one was open for 4% of the time, Pallas kernels for 0%

commit v1 on v0

v1 whole, which is shorter than its diff:
```python
import jax
import jax.numpy as jnp
from jax import lax
from jax.experimental import pallas as pl
from jax.experimental.pallas import tpu as pltpu
from jax.sharding import PartitionSpec as P

NX, NY, NZ = 4, 4, 16
NP = NX * NY
MESH = pl.DeviceIdType.MESH
VM = pl.BlockSpec(memory_space=pltpu.VMEM)


def place():
    dp = lax.axis_index("dp")
    fr = lax.axis_index("frame")
    return lax.div(dp, 2), lax.rem(dp, 2), lax.div(fr, NX), lax.rem(fr, NX)


def device(y, core, z, x):
    return (y * 2 + core, z * NX + x)


def push(src, dst, send, recv, to):
    return pltpu.make_async_remote_copy(
        src_ref=src, dst_ref=dst, send_sem=send, recv_sem=recv, device_id=to, device_id_type=MESH
    )


def greet(barrier, to):
    pl.semaphore_signal(barrier, inc=1, device_id=to, device_id_type=MESH)


def gather_kernel(w_ref, full, pair, pair_rows, zbuf, rows, send0, recv0, send1, recv1, send2, recv2, send3, recv3, send4, recv4):
    y, core, z, x = place()
    other = 1 - core
    partner = device(y, other, z, x)

    barrier = pltpu.get_barrier_semaphore()
    greet(barrier, partner)

    @pl.loop(1, NZ)
    def _(k):
        greet(barrier, device(y, core, lax.rem(z + k, NZ), x))

    @pl.loop(1, NX)
    def _(k):
        greet(barrier, device(y, core, z, lax.rem(x + k, NX)))

    @pl.loop(1, NY)
    def _(k):
        greet(barrier, device(lax.rem(y + k, NY), core, z, x))

    pl.semaphore_wait(barrier, 1 + NZ - 1 + NX - 1 + NY - 1)

    swap = push(w_ref.at[other], pair.at[core], send0, recv0, partner)
    swap.start()
    pair[core] = w_ref[core]
    swap.wait()
    pair_rows[...] = jnp.zeros_like(pair_rows)
    pair_rows[0:3] = pair[0, 0:3].astype(jnp.float32)
    pair_rows[3:6] = pair[1, 0:3].astype(jnp.float32)
    zbuf[z] = pair_rows[...].astype(jnp.bfloat16)

    def along_z(k):
        return push(zbuf.at[z], zbuf.at[z], send1.at[k], recv1.at[k], device(y, core, lax.rem(z + k, NZ), x))

    @pl.loop(1, NZ)
    def _(k):
        along_z(k).start()

    @pl.loop(1, NZ)
    def _(k):
        along_z(k).wait_recv()

    for k in range(NZ):
        rows[6 * k:6 * k + 6] = zbuf[k, 0:6].astype(jnp.float32)
    full[core, y, x] = rows[...].astype(jnp.bfloat16)

    def second(k):
        to = device(lax.rem(y + k * other, NY), core, z, lax.rem(x + k * core, NX))
        block = full.at[core, y, x]
        return push(block, block, send2.at[k], recv2.at[k], to)

    def third(k, yy, xx, turn):
        to = device(lax.rem(y + k * core, NY), core, z, lax.rem(x + k * other, NX))
        block = full.at[core, yy, xx]
        return push(block, block, send3.at[turn, k], recv3.at[turn, k], to)

    def fourth(yy, xx):
        block = full.at[core, yy, xx]
        return push(block, block, send4.at[yy, xx], recv4.at[yy, xx], partner)

    def late(k):
        return lax.rem(y + (4 - k) * other, NY), lax.rem(x + (4 - k) * core, NX)

    @pl.loop(1, 4)
    def _(k):
        second(k).start()

    @pl.loop(1, 4)
    def _(k):
        third(k, y, x, 0).start()

    fourth(y, x).start()

    @pl.loop(1, 4)
    def _(turn):
        second(turn).wait_recv()
        yy, xx = late(turn)

        @pl.loop(1, 4)
        def _(k):
            third(k, yy, xx, turn).start()

        fourth(yy, xx).start()

    @pl.loop(0, 4)
    def _(turn):
        yy, xx = late(turn)

        @pl.loop(1, 4)
        def _(k):
            third(k, yy, xx, turn).wait_recv()
            fourth(lax.rem(yy + (4 - k) * core, NY), lax.rem(xx + (4 - k) * other, NX)).start()

    @pl.loop(0, NP)
    def _(i):
        fourth(lax.div(i, NX), lax.rem(i, NX)).wait()

    @pl.loop(1, NZ)
    def _(k):
        along_z(k).wait_send()

    @pl.loop(1, 4)
    def _(k):
        second(k).wait_send()

    @pl.loop(0, 4)
    def _(turn):
        yy, xx = late(turn)

        @pl.loop(1, 4)
        def _(k):
            third(k, yy, xx, turn).wait_send()


def gather_weights(shard):
    dma = pltpu.SemaphoreType.DMA
    return pl.pallas_call(
        gather_kernel,
        out_shape=jax.ShapeDtypeStruct((2, NY, NX, 6 * NZ, 768), jnp.bfloat16),
        in_specs=[VM],
        out_specs=VM,
        scratch_shapes=[
            pltpu.VMEM((2, 8, 768), jnp.bfloat16),
            pltpu.VMEM((8, 768), jnp.float32),
            pltpu.VMEM((NZ, 8, 768), jnp.bfloat16),
            pltpu.VMEM((6 * NZ, 768), jnp.float32),
            dma, dma, dma((NZ,)), dma((NZ,)), dma((4,)), dma((4,)),
            dma((4, 4)), dma((4, 4)), dma((NY, NX)), dma((NY, NX)),
        ],
        compiler_params=pltpu.CompilerParams(collective_id=0, has_side_effects=True, vmem_limit_bytes=40 << 20),
        name="gather_weights",
    )(shard)


def total_kernel(x_ref, out, r0, r1, r2, acc, done, send0, recv0, send1, recv1, send2, recv2, send3, recv3, send4, recv4, send5, recv5):
    y, core, z, x = place()
    me = y * NX + x
    other = 1 - core
    partner = device(y, other, z, x)

    def plane(k):
        p = lax.rem(me + k, NP)
        return p, device(lax.div(p, NX), core, z, lax.rem(p, NX))

    def column(k):
        zz = lax.rem(z + k, NZ)
        return zz, device(y, core, zz, x)

    barrier = pltpu.get_barrier_semaphore()
    greet(barrier, partner)

    @pl.loop(1, NP)
    def _(k):
        greet(barrier, plane(k)[1])

    @pl.loop(1, NZ)
    def _(k):
        greet(barrier, column(k)[1])

    pl.semaphore_wait(barrier, 1 + NP - 1 + NZ - 1)

    swap = push(x_ref.at[other], r0, send0, recv0, partner)
    swap.start()
    swap.wait()

    @pl.loop(0, NP)
    def _(p):
        acc[p] = x_ref[core, p] + r0[p]

    def first(k):
        p, to = plane(k)
        return push(acc.at[p], r1.at[me], send1.at[k], recv1.at[k], to)

    @pl.loop(1, NP)
    def _(k):
        first(k).start()

    r1[me] = acc[me]

    @pl.loop(1, NP)
    def _(k):
        first(k).wait()

    part = r1[0]
    for p in range(1, NP):
        part = part + r1[p]
    acc[me] = part

    def second(k):
        zz, to = column(k)
        return push(acc.at[me, zz], r2.at[z], send2.at[k], recv2.at[k], to)

    @pl.loop(1, NZ)
    def _(k):
        second(k).start()

    r2[z] = acc[me, z]

    @pl.loop(1, NZ)
    def _(k):
        second(k).wait()

    whole = r2[0]
    for p in range(1, NZ):
        whole = whole + r2[p]
    done[...] = whole
    out[core, me, z] = whole

    def third(k):
        return push(done, out.at[core, me, z], send3.at[k], recv3.at[k], column(k)[1])

    @pl.loop(1, NZ)
    def _(k):
        third(k).start()

    @pl.loop(1, NZ)
    def _(k):
        third(k).wait()

    def fourth(k):
        return push(out.at[core, me], out.at[core, me], send4.at[k], recv4.at[k], plane(k)[1])

    @pl.loop(1, NP)
    def _(k):
        fourth(k).start()

    def fifth(p):
        return push(out.at[core, p], out.at[core, p], send5.at[p], recv5.at[p], partner)

    fifth(me).start()

    @pl.loop(1, NP)
    def _(k):
        fourth(k).wait()
        fifth(lax.rem(me + NP - k, NP)).start()

    @pl.loop(0, NP)
    def _(p):
        fifth(p).wait()


def total(parts):
    dma = pltpu.SemaphoreType.DMA
    f32 = jnp.float32
    return pl.pallas_call(
        total_kernel,
        out_shape=jax.ShapeDtypeStruct((2, NP, NZ, 2, 128), f32),
        in_specs=[VM],
        out_specs=VM,
        scratch_shapes=[
            pltpu.VMEM((NP, NZ, 2, 128), f32),
            pltpu.VMEM((NP, NZ, 2, 128), f32),
            pltpu.VMEM((NZ, 2, 128), f32),
            pltpu.VMEM((NP, NZ, 2, 128), f32),
            pltpu.VMEM((2, 128), f32),
            dma, dma, dma((NP,)), dma((NP,)), dma((NZ,)), dma((NZ,)),
            dma((NZ,)), dma((NZ,)), dma((NP,)), dma((NP,)), dma((NP,)), dma((NP,)),
        ],
        compiler_params=pltpu.CompilerParams(collective_id=1, has_side_effects=True, vmem_limit_bytes=40 << 20),
        name="total",
    )(parts)

HEADS = 8


def norm_rows(values):
    center = values - jnp.mean(values, -1, keepdims=True)
    inverse = lax.rsqrt(jnp.mean(center * center, -1, keepdims=True) + 1e-05)
    return (center * inverse, inverse)


def attend(query, key_rows, live_keys, gradient, head_count):
    inner_width = query.shape[1]
    head_size = inner_width // head_count
    query_heads = query.reshape(-1, head_count, head_size)
    key_heads = key_rows[:, :inner_width].reshape(-1, head_count, head_size)
    value_heads = key_rows[:, inner_width:].reshape(-1, head_count, head_size)
    scores = jnp.einsum("qhd,khd->hqk", query_heads, key_heads, preferred_element_type=jnp.float32)
    scores = jnp.where(live_keys[None, None, :], scores, -jnp.inf)
    weights = jax.nn.softmax(scores, axis=-1)
    weights_low = weights.astype(jnp.bfloat16)
    attended = jnp.einsum(
        "hqk,khd->qhd", weights_low, value_heads, preferred_element_type=jnp.float32
    )
    attended = attended.reshape(-1, inner_width).astype(jnp.bfloat16)
    grad_heads = gradient.reshape(-1, head_count, head_size)
    grad_weights = jnp.einsum(
        "qhd,khd->hqk", grad_heads, value_heads, preferred_element_type=jnp.float32
    )
    grad_scores = weights * (grad_weights - jnp.sum(weights * grad_weights, -1, keepdims=True))
    grad_scores = grad_scores.astype(jnp.bfloat16)
    grad_query = jnp.einsum(
        "hqk,khd->qhd", grad_scores, key_heads, preferred_element_type=jnp.float32
    )
    grad_key = jnp.einsum(
        "hqk,qhd->khd", grad_scores, query_heads, preferred_element_type=jnp.float32
    )
    grad_value = jnp.einsum(
        "hqk,qhd->khd", weights_low, grad_heads, preferred_element_type=jnp.float32
    )
    grad_keyval = jnp.concatenate(
        [grad_key.reshape(-1, inner_width), grad_value.reshape(-1, inner_width)], axis=1
    )
    return (attended, grad_query.reshape(-1, inner_width), grad_keyval)


def natural_order():
    place = jnp.arange(384)
    gathered = place // 96, place % 96 // 6, place % 6 // 3, place % 3
    natural = gathered[2] * 192 + gathered[1] * 12 + gathered[0] * 3 + gathered[3]
    return (jnp.arange(384)[:, None] == natural[None, :]).astype(jnp.bfloat16)


def reorder(rows, order, side):
    dims = (((1,), (side,)), ((), ()))
    blocks = rows.reshape(-1, 384)
    return lax.dot_general(blocks, order, dims, preferred_element_type=jnp.float32).astype(rows.dtype).reshape(rows.shape)


def reorder_precise(rows, order):
    blocks = rows.reshape(-1, 384)
    result = 0.0
    for _ in range(3):
        part = blocks.astype(jnp.bfloat16)
        blocks = blocks - part.astype(jnp.float32)
        result = result + lax.dot_general(part, order, (((1,), (1,)), ((), ())), preferred_element_type=jnp.float32)
    return result.reshape(rows.shape)


def both(left, right, first, second, side):
    dims = (((1,), (side,)), ((), ()))
    return (
        lax.dot_general(left, first, dims, preferred_element_type=jnp.float32),
        lax.dot_general(right, second, dims, preferred_element_type=jnp.float32),
    )


def precise_both(left, right, first, second):
    result = 0.0
    for _ in range(2):
        high = left.astype(jnp.bfloat16), right.astype(jnp.bfloat16)
        one, two = both(*high, first, second, 1)
        result = result + one + two
        left, right = left - high[0].astype(jnp.float32), right - high[1].astype(jnp.float32)
    return result


def body(
    frame_features,
    frame_owner,
    latents,
    latent_gain,
    media_gain,
    query_proj,
    keyval_proj,
    grad_output,
):
    owners = lax.axis_size("frame")
    inner = query_proj.shape[1]
    score_scale = (inner // HEADS) ** (-0.5)
    half = inner // 2
    shard = jnp.stack(
        [
            jnp.concatenate([keyval_proj[:, :inner], query_proj[:, :half]], axis=1),
            jnp.concatenate([keyval_proj[:, inner:], query_proj[:, half:]], axis=1),
        ]
    )
    full = gather_weights(jnp.pad(shard, ((0, 0), (0, 5), (0, 0)))).reshape(2, 1536, 768)
    key_proj, value_proj = full[0, :, :inner], full[1, :, :inner]
    query_left, query_right = full[0, :, inner:], full[1, :, inner:]
    order = natural_order()

    def project(rows, first, second):
        return jnp.concatenate(both(rows, rows, first, second, 0), axis=1)

    latent_hat, latent_inv = norm_rows(latents)
    latent_norm = reorder((latent_hat * latent_gain).astype(jnp.bfloat16), order, 0)
    query = (project(latent_norm, query_left, query_right) * score_scale).astype(jnp.bfloat16)
    latent_keyval = project(latent_norm, key_proj, value_proj).astype(jnp.bfloat16)
    frames = frame_features[0]
    frame_count, frame_tokens, width = frames.shape
    media_hat, _ = norm_rows(frames.astype(jnp.float32).reshape(-1, width))
    media_norm = reorder((media_hat * media_gain).astype(jnp.bfloat16), order, 0)
    media_keyval = project(media_norm, key_proj, value_proj).astype(jnp.bfloat16)
    route = frame_owner[0, :, 0]
    selected = route[None, :] == jnp.arange(owners, dtype=jnp.int32)[:, None]
    slot_live = jnp.sum(selected.astype(jnp.int32), axis=1).reshape(owners, 1)
    selector = selected.astype(jnp.bfloat16)
    packed = jnp.dot(selector, media_keyval.reshape(frame_count, -1), preferred_element_type=jnp.float32)
    received = lax.all_to_all(
        packed.astype(jnp.bfloat16).reshape(owners, frame_tokens, -1), "frame", split_axis=0, concat_axis=0, tiled=True
    )
    live_slots = lax.all_to_all(slot_live, "frame", split_axis=0, concat_axis=0, tiled=True)
    media_rows = owners * frame_tokens
    key_rows = jnp.concatenate([received.reshape(media_rows, -1), latent_keyval], axis=0)
    live_keys = jnp.concatenate(
        [jnp.repeat(live_slots.reshape(-1) > 0, frame_tokens), jnp.ones((latents.shape[0],), bool)]
    )
    attended, grad_query, grad_keyval = attend(query, key_rows, live_keys, grad_output[0, 0], HEADS)
    grad_media = grad_keyval[:media_rows].astype(jnp.bfloat16).reshape(owners, frame_tokens, -1)
    returned = lax.all_to_all(grad_media, "frame", split_axis=0, concat_axis=0, tiled=True)
    frame_rows = lax.dot_general(
        selector, returned.reshape(owners, -1), (((0,), (0,)), ((), ())), preferred_element_type=jnp.float32
    )
    frame_grad = frame_rows.astype(jnp.bfloat16).reshape(frame_count * frame_tokens, -1)
    from_key, from_value = both(frame_grad[:, :inner], frame_grad[:, inner:], key_proj, value_proj, 1)
    grad_norm = reorder((from_key + from_value).astype(jnp.bfloat16), order, 1)
    media_term = jnp.sum(grad_norm.astype(jnp.float32) * media_hat, axis=0)
    sums = jnp.concatenate([grad_query * score_scale, grad_keyval[media_rows:]], axis=1)
    flat = jnp.concatenate([sums.reshape(-1), media_term, jnp.zeros((131072 - sums.size - width,), jnp.float32)])
    flat = total(flat.reshape(2, NP, NZ, 2, 128)).reshape(-1)
    sums, media_gain_grad = flat[: sums.size].reshape(sums.shape), flat[sums.size : sums.size + width]
    grad_latent_norm = precise_both(sums[:, :half], sums[:, half:inner], query_left, query_right)
    grad_latent_norm = grad_latent_norm + precise_both(
        sums[:, inner : 2 * inner], sums[:, 2 * inner :], key_proj, value_proj
    )
    grad_latent_norm = reorder_precise(grad_latent_norm, order)
    latent_gain_grad = jnp.sum(grad_latent_norm * latent_hat, axis=0)
    grad_hat = grad_latent_norm * latent_gain
    latent_grad = latent_inv * (
        grad_hat
        - jnp.mean(grad_hat, -1, keepdims=True)
        - latent_hat * jnp.mean(grad_hat * latent_hat, -1, keepdims=True)
    )
    return (attended[None, None], latent_grad, latent_gain_grad, media_gain_grad)


def solution(mesh):
    placed = (
        P("dp", "frame", None, None),
        P("dp", "frame", None),
        P(),
        P(),
        P(),
        P(("dp", "frame"), None),
        P(("dp", "frame"), None),
        P("dp", "frame", None, None),
    )
    return jax.shard_map(
        body,
        mesh=mesh,
        in_specs=placed,
        out_specs=(P("dp", "frame", None, None), P(), P(), P()),
        check_vma=False,
    )
```

time: 1080 us -> 292 us (0.27)
  waiting for transfers between devices: 852 us -> 70.7 us
  blocking collectives: 105 us -> 0 us
  Pallas kernels: 0 us -> 87.2 us
  between operations: 14.1 us -> 1.41 us
  matrix products: 28.6 us -> 40.3 us
    psum x1 -> x0, waiting for transfers between devices: 481 us -> none  [body(): lax.psum((grad_query * score_scale, grad_keyval[media_rows:], media_term)...]
    all_gather x2 -> x0, waiting for transfers between devices: 364 us -> none  [the longest x1 193 us: body(): lax.all_gather(keyval_proj, ('dp', 'frame'), axis=0, tiled=True)]
    psum x1 -> x0, blocking collectives: 105 us -> none  [body(): lax.psum((grad_query * score_scale, grad_keyval[media_rows:], media_term)...]
    pallas_call x0 -> x2, Pallas kernels: none -> 87.2 us  [the longest x1 47.6 us: gather_weights(): pl.pallas_call(gather_kernel, out_shape=jax.ShapeDtypeStruct((2, NY, NX,...]
    all_to_all x2, waiting for transfers between devices: 0.01 us -> 70.7 us  [the longest x1 36.4 us: body(): lax.all_to_all(grad_media, 'frame', split_axis=0, concat_axis=0, tiled=True)]
    unnamed x60 -> x67, local copies, waits for them, and re-layouts: 22.1 us -> 9.42 us
    dot_general x10 -> x24, matrix products: 16.5 us -> 27.8 us  [the longest x8 11.5 us: both(): lax.dot_general(left, first, dims, preferred_element_type=jnp.float32)]
  transfers between devices with their start and end apart: 6 -> 3, of which waited for: 4 -> 2; matrix products, arithmetic and copies ran while one was open for 4% -> 16% of each run, Pallas kernels for 0% -> 16%
where the time goes in v1:
time: 292 us; the launch traced here: 290 us
  Pallas kernels  87.2 us (30%)
  waiting for transfers between devices  70.7 us (24%)
  starting transfers between devices  41.7 us (14%)
  matrix products  40.3 us (14%)
  local copies, waits for them, and re-layouts  38.1 us (13%)
  other arithmetic  10.8 us (4%)
    pallas_call x1, Pallas kernels, gather_weights(): pl.pallas_call(gather_kernel, out_shape=jax.ShapeDtypeStruct((2, NY, NX,...  47.6 us
    pallas_call x1, Pallas kernels, total(): pl.pallas_call(total_kernel, out_shape=jax.ShapeDtypeStruct((2, NP, NZ, 2...  39.6 us
    all_to_all x1, waiting for transfers between devices, body(): lax.all_to_all(grad_media, 'frame', split_axis=0, concat_axis=0, tiled=True)  36.4 us
    all_to_all x1, waiting for transfers between devices, body(): lax.all_to_all(packed.astype(jnp.bfloat16).reshape(owners, frame_tokens,...  34.2 us
    all_to_all x1, starting transfers between devices, body(): lax.all_to_all(slot_live, 'frame', split_axis=0, concat_axis=0, tiled=True)  19.4 us
    all_to_all x1, starting transfers between devices, body(): lax.all_to_all(packed.astype(jnp.bfloat16).reshape(owners, frame_tokens,...  13.9 us
    dot_general x8, matrix products, both(): lax.dot_general(left, first, dims, preferred_element_type=jnp.float32)  11.5 us
    dot_general x8, matrix products, both(): lax.dot_general(right, second, dims, preferred_element_type=jnp.float32)  10 us
  transfers between devices with their start and end apart: 3, of which 2 were waited for; matrix products, arithmetic and copies ran while one was open for 16% of the time, Pallas kernels for 16%

profile of v1, /device:TPU:1, one launch (start us, length us, event | category | flops | bytes accessed | tf_op | source)
XLA Modules:
  0.0 290.3 jit_solution(2904962427454717197)
XLA Ops:
  0.6 0.8 convert_reduce_fusion.1
  2.2 19.4 %all-to-all-start.1 = ((s32[64,1,1]{2,1,0:T(1,128)}), s32[64,1,1]{2,1,0:T(1,128)}, u32[]{:S(2)}, u32[]{:S(2)}) async-start(s32[64,1,1]{2,1,0:T(1,128)} %copy.57), calls=%async_computation.1 | async-start | bytes 65536 | tf_op jit(solution)/shard_map/all_to_all | solution.py:426
  21.6 1.3 convert_reduce_fusion
  23.0 1.5 multiply_reduce_fusion
  25.6 1.4 mul.174
  26.9 2.8 mul.175
  29.7 2.1 convolution_convert_fusion.3
  32.4 47.6 %gather_weights.1 = bf16[2,4,4,96,768]{4,3,2,1,0:T(8,128)(2,1)S(1)} custom-call(bf16[2,8,768]{2,1,0:T(8,128)(2,1)S(1)} %fusion.44.w_ref), custom_call_target="tpu_custom_call" | custom-call | tf_op jit(solution)/shard_map/gather_weights/pallas_call | solution.py:150
  80.5 1.5 copy-done
  83.9 1.6 copy.69
  85.5 13.9 %all-to-all-start = ((bf16[64,8,1024]{2,1,0:T(8,128)(2,1)}), bf16[64,8,1024]{2,1,0:T(8,128)(2,1)S(1)}, u32[]{:S(2)}, u32[]{:S(2)}) async-start(bf16[64,8,1024]{2,1,0:T(8,128)(2,1)} %bitcast.38), calls=%async_computation | async-start | bytes 2097152 | tf_op jit(solution)/shard_map/all_to_all | solution.py:423
  101.4 1.8 convolution_convert_fusion.8
  103.2 1.8 convolution_convert_fusion.9
  105.2 2.7 slice_bitcast_fusion.13
  107.8 1.4 copy.58
  109.2 2.3 copy.59
  111.6 1.2 fusion.89
  112.7 2.3 fusion.90
  115.0 2.0 compare_reduce_fusion
  117.7 34.2 %all-to-all-done = bf16[64,8,1024]{2,1,0:T(8,128)(2,1)S(1)} async-done(((bf16[64,8,1024]{2,1,0:T(8,128)(2,1)}), bf16[64,8,1024]{2,1,0:T(8,128)(2,1)S(1)}, u32[]{:S(2)}, u32[]{:S(2)}) %all-to-all-start) | async-done | bytes 1048608 | tf_op jit(solution)/shard_map/all_to_all | solution.py:423
  152.5 1.0 pad_maximum_fusion.1
  153.5 1.6 fusion.86
  155.1 2.2 fusion.26
  157.3 1.8 copy.64
  159.1 1.9 multiply_reduce_fusion.1
  162.0 1.5 fusion.73
  163.5 1.7 copy.63
  165.2 1.2 fusion.10
  166.4 8.5 %all-to-all-start.2 = ((bf16[64,8,1024]{2,1,0:T(8,128)(2,1)}), bf16[64,8,1024]{2,1,0:T(8,128)(2,1)}, u32[]{:S(2)}, u32[]{:S(2)}) async-start(bf16[64,8,1024]{2,1,0:T(8,128)(2,1)} %fusion.10), calls=%async_computation.2 | async-start | bytes 2097152 | tf_op jit(solution)/shard_map/all_to_all | solution.py:434
  175.5 1.5 mul.198
  176.9 1.9 mul.199
  178.8 3.1 %convolution_convert_fusion.7 = bf16[8,64,64]{2,1,0:T(8,128)(2,1)} fusion(bf16[576,8,64]{0,2,1:T(8,128)(2,1)} %bitcast.129, f32[8,64]{1,0:T(8,128)} %copy-done.25, bf16[576,8,64]{0,2,1:T(8,128)(2,1)} %bitcast.125, pred[576]{0:T(1024)(128)(4,1)} %concatenate.38, f32[64,4,64]{2,0,1:T(8,128)} %fusion.90, f32[64,4,64]{2,0,1:T(8,128)} %fusion.89), kind=kOutput, calls=%fused_computation.42 | convolution fusion | flops 76809280 | bytes 1378880 | tf_op jit(solution)/shard_map/hqk,khd->qhd/dot_general | solution.py:315
  181.9 1.6 copy.66
  183.5 2.3 convolution_multiply_fusion
  185.9 1.7 copy.65
  187.6 0.9 copy-done.13
  189.3 36.4 %all-to-all-done.2 = bf16[64,8,1024]{2,1,0:T(8,128)(2,1)} async-done(((bf16[64,8,1024]{2,1,0:T(8,128)(2,1)}), bf16[64,8,1024]{2,1,0:T(8,128)(2,1)}, u32[]{:S(2)}, u32[]{:S(2)}) %all-to-all-start.2) | async-done | bytes 1048608 | tf_op jit(solution)/shard_map/all_to_all | solution.py:434
  225.7 1.8 copy.70
  228.2 2.0 fusion.12
  230.2 2.0 fusion.1
  232.7 1.8 fusion.9
  234.5 1.5 reshape.257
  237.1 39.6 %total.1 = f32[2,16,16,2,128]{4,3,2,1,0:T(2,128)S(1)} custom-call(f32[2,16,16,2,128]{4,3,2,1,0:T(2,128)S(1)} %bitcast.114), custom_call_target="tpu_custom_call" | custom-call | tf_op jit(solution)/shard_map/total/pallas_call | solution.py:278
  277.5 2.1 fusion.11
  279.6 1.5 fusion.15
  281.1 2.0 convolution_add_fusion.3
  283.2 2.0 convolution_add_fusion.2
  289.4 0.9 subtract_multiply_fusion
  (130 shorter events, 17.3 us)
Async XLA Ops:
  0.6 23.9 %copy-start.1 = (bf16[1,32,8,1536]{3,2,1,0:T(8,128)(2,1)S(1)}, bf16[1,32,8,1536]{3,2,1,0:T(8,128)(2,1)}, u32[]{:S(2)}) copy-start(bf16[1,32,8,1536]{3,2,1,0:T(8,128)(2,1)} %param.8) | copy-start | bytes 2359300
  2.2 83.3 %all-to-all-start.1 = ((s32[64,1,1]{2,1,0:T(1,128)}), s32[64,1,1]{2,1,0:T(1,128)}, u32[]{:S(2)}, u32[]{:S(2)}) async-start(s32[64,1,1]{2,1,0:T(1,128)} %copy.57), calls=%async_computation.1 | async-start | bytes 65536 | tf_op jit(solution)/shard_map/all_to_all | solution.py:426
  23.0 2.0 copy-start.26
  23.0 2.0 copy-start.19
  23.0 2.0 copy-start.20
  25.1 4.6 %copy-start.17 = (f32[256]{0:T(256)}, f32[256]{0:T(256)S(1)}, u32[]{:S(2)}) copy-start(f32[256]{0:T(256)S(1)} %rsqrt.20) | copy-start | bytes 3076
  80.0 2.1 copy-start
  82.6 0.7 copy-start.27
  85.4 13.9 %copy-start.2 = (f32[64,1536]{1,0:T(8,128)S(1)}, f32[64,1536]{1,0:T(8,128)}, u32[]{:S(2)}) copy-start(f32[64,1536]{1,0:T(8,128)} %param.10) | copy-start | bytes 1179652
  85.4 14.3 %copy-start.14 = (f32[1536]{0:T(1024)S(1)}, f32[1536]{0:T(1024)}, u32[]{:S(2)}) copy-start(f32[1536]{0:T(1024)} %param.11) | copy-start | bytes 18436
  85.5 66.5 %all-to-all-start = ((bf16[64,8,1024]{2,1,0:T(8,128)(2,1)}), bf16[64,8,1024]{2,1,0:T(8,128)(2,1)S(1)}, u32[]{:S(2)}, u32[]{:S(2)}) async-start(bf16[64,8,1024]{2,1,0:T(8,128)(2,1)} %bitcast.38), calls=%async_computation | async-start | bytes 2097152 | tf_op jit(solution)/shard_map/all_to_all | solution.py:423
  99.3 1.2 copy-start.16
  99.5 3.7 %copy-start.21 = (f32[64]{0:T(128)}, f32[64]{0:T(128)S(1)}, u32[]{:S(2)}) copy-start(f32[64]{0:T(128)S(1)} %broadcast_multiply_fusion.3) | copy-start | bytes 772
  99.7 3.4 %copy-start.23 = (f32[64]{0:T(128)}, f32[64]{0:T(128)S(1)}, u32[]{:S(2)}) copy-start(f32[64]{0:T(128)S(1)} %add_rsqrt_fusion.1) | copy-start | bytes 772
  152.5 1.0 copy-start.9
  152.5 1.0 copy-start.11
  152.5 1.0 copy-start.29
  153.5 3.8 %copy-start.4 = (bf16[576,512]{0,1:T(8,128)(2,1)}, bf16[576,512]{0,1:T(8,128)(2,1)S(1)}, u32[]{:S(2)}) copy-start(bf16[576,512]{0,1:T(8,128)(2,1)S(1)} %get-tuple-element.28) | copy-start | bytes 1769476
  153.5 1.6 copy-start.15
  155.1 5.9 %copy-start.25 = (f32[8,64]{1,0:T(8,128)}, f32[8,64]{1,0:T(8,128)S(1)}, u32[]{:S(2)}) copy-start(f32[8,64]{1,0:T(8,128)S(1)} %get-tuple-element.34) | copy-start | bytes 6148
  157.3 1.8 copy-start.8
  159.1 1.9 copy-start.7
  161.0 0.9 copy-start.10
  161.0 1.0 copy-start.12
  162.0 1.5 copy-start.3
  166.4 59.4 %all-to-all-start.2 = ((bf16[64,8,1024]{2,1,0:T(8,128)(2,1)}), bf16[64,8,1024]{2,1,0:T(8,128)(2,1)}, u32[]{:S(2)}, u32[]{:S(2)}) async-start(bf16[64,8,1024]{2,1,0:T(8,128)(2,1)} %fusion.10), calls=%async_computation.2 | async-start | bytes 2097152 | tf_op jit(solution)/shard_map/all_to_all | solution.py:434
  187.6 0.9 copy-start.13
  188.5 39.0 %copy-start.28 = (s32[1,32,1]{1,2,0:T(1,128)S(1)}, s32[1,32,1]{1,2,0:T(1,128)}, u32[]{:S(2)}) copy-start(s32[1,32,1]{1,2,0:T(1,128)} %param.9) | copy-start | bytes 388
  234.5 1.5 copy-start.18
  236.1 1.0 copy-start.6
  236.1 49.1 %slice-start = ((s8[4718592]{0:T(1024)(128)(4,1)}), s8[524288]{0:T(1024)(128)(4,1)S(1)}, s32[]{:S(2)}) async-start(s8[4718592]{0:T(1024)(128)(4,1)} %bitcast.108), calls=%async_computation.3 | async-start | bytes 1048576
  277.5 7.7 %slice-start.1 = ((s8[4718592]{0:T(1024)(128)(4,1)}), s8[4194304]{0:T(1024)(128)(4,1)S(1)}, s32[]{:S(2)}) async-start(s8[4718592]{0:T(1024)(128)(4,1)} %bitcast.108), calls=%async_computation.4 | async-start | bytes 8388608
  286.9 1.0 copy-start.5
  287.3 1.3 copy-start.22
  287.3 1.3 copy-start.24

commit v2 on v0

v2 whole, which is shorter than its diff:
```python
import jax
import jax.numpy as jnp
import numpy as np
from jax import lax
from jax.experimental import pallas as pl
from jax.experimental.pallas import tpu as pltpu
from jax.sharding import PartitionSpec as P

NX, NY, NZ = 4, 4, 16
NP = NX * NY
HEADS, HEAD, INNER, WIDTH, LAT = 8, 64, 512, 1536, 64
TOK, FRAMES = 8, 32
ROWS = FRAMES * TOK
KEYS = NX * TOK
SLOTS = NZ * TOK
SEND = 2 * INNER + 128
DEAD = -1e30
MESH = pl.DeviceIdType.MESH
F32, BF16 = jnp.float32, jnp.bfloat16
DMA = pltpu.SemaphoreType.DMA


def gathered_order():
    place = np.arange(384)
    natural = place % 6 // 3 * 192 + place % 96 // 6 * 12 + place // 96 * 3 + place % 3
    return (np.arange(384)[:, None] == natural[None, :]).astype(np.float32)


def sample_order():
    place = np.arange(NZ * KEYS)
    source = place % KEYS // TOK * SLOTS + place // KEYS * TOK + place % TOK
    return (source[:, None] == np.arange(NZ * KEYS)[None, :]).astype(np.float32)


def dot(left, right, dims=((1,), (0,))):
    return lax.dot_general(left, right, (dims, ((), ())), preferred_element_type=F32)


def dot_nt(left, right):
    return dot(left, right, ((1,), (1,)))


def dot_tn(left, right):
    return dot(left, right, ((0,), (0,)))


def norm_rows(values):
    center = values - jnp.mean(values, -1, keepdims=True)
    inverse = lax.rsqrt(jnp.mean(center * center, -1, keepdims=True) + 1e-05)
    return center * inverse, inverse


def iota(shape, dim):
    return lax.broadcasted_iota(jnp.int32, shape, dim)


def by_head(rows):
    shape = (HEADS * LAT, INNER)
    same = (iota(shape, 0) >> 6) == (iota(shape, 1) >> 6)
    return jnp.where(same, jnp.concatenate([rows.astype(F32)] * HEADS, axis=0), 0.0).astype(BF16)


def head_blocks(left, right):
    blocks = []
    for pair in range(HEADS // 2):
        lanes = slice(pair * 128, pair * 128 + 128)
        both = dot_tn(left[:, lanes], right[:, lanes])
        blocks.append(jnp.where(iota((HEAD, 128), 1) < HEAD, both[:HEAD], both[HEAD:]))
    return jnp.concatenate(blocks, axis=1)


def push(src, dst, send, recv, to):
    return pltpu.make_async_remote_copy(
        src_ref=src, dst_ref=dst, send_sem=send, recv_sem=recv, device_id=to, device_id_type=MESH
    )


INPUTS = ("shard", "frames", "latents", "latent_gain", "media_gain", "route_lane", "route_rows", "grad", "order", "sorting")
OUTPUTS = ("attended", "latent_grad", "latent_gain_grad", "media_gain_grad")
BUFFERS = dict(
    pair=((2, 8, 768), BF16),
    pair_rows=((8, 768), F32),
    zbuf=((NZ, 8, 768), BF16),
    rows=((6 * NZ, 768), F32),
    wkv=((2, 2, NY, NX, 6 * NZ, 256), BF16),
    wq=((2, 2, NY, NX, 6 * NZ, 128), BF16),
    gob=((NZ, LAT, INNER), BF16),
    hat=((ROWS, WIDTH), F32),
    normed=((ROWS, WIDTH), BF16),
    kv=((ROWS, 2 * INNER), BF16),
    slots=((NX, SLOTS, SEND), BF16),
    got=((NX, SLOTS, SEND), BF16),
    kvs=((NZ, KEYS, SEND), BF16),
    lat_normed=((LAT, WIDTH), BF16),
    lat_kv=((LAT, 2 * INNER), BF16),
    qrow=((HEADS * LAT, INNER), BF16),
    gorow=((NZ, HEADS * LAT, INNER), BF16),
    scores=((NZ, KEYS, INNER), F32),
    gprob=((NZ, KEYS, INNER), F32),
    lat_scores=((LAT, INNER), F32),
    lat_gprob=((LAT, INNER), F32),
    stat=((NZ, 3, 1, INNER), F32),
    stat_got=((NZ, 3, 1, INNER), F32),
    stat_own=((3, 1, INNER), F32),
    stat_all=((NZ, 3, 1, INNER), F32),
    gs=((NZ, KEYS, INNER), BF16),
    gkv=((NZ, KEYS, 2 * INNER), BF16),
    back=((NX, SLOTS, 2 * INNER), BF16),
    back_got=((NX, SLOTS, 2 * INNER), BF16),
    part=((NZ, LAT, INNER), F32),
    lat_out=((4, LAT, INNER), F32),
    ring_out=((2, 9, LAT, INNER), BF16),
    ring_in=((2, 9, LAT, INNER), BF16),
    sums=((2, NP, 3, 8, 128), F32),
    sums_core=((NP, 3, 8, 128), F32),
    sums_plane=((NP, 3, 8, 128), F32),
    media=((NP, 1, 128), F32),
    media_core=((NP, 1, 128), F32),
    media_plane=((NP, 1, 128), F32),
    chunk=((4, 8, 128), F32),
    chunk_got=((4, NZ, 8, 128), F32),
    whole=((2, NP, 4, 8, 128), F32),
)
SEMS = dict(
    swap=(1,), along_z=(NZ,), go=(2, 9), kv2=(2, 4), kv3=(2, 4), kv4=(2, 4), q2=(2, 4), q3=(2, 4), q4=(2, 4),
    out_x=(4,), back_x=(4,), stat_to=(NZ,), stat_from=(NZ,), ring=(2, 9),
    sum_core=(1,), sum_plane=(NP,), med_core=(1,), med_plane=(NP,), red_z=(4, NZ), all_z=(4, NZ), all_plane=(NP,), all_core=(NP,),
)


class Refs:
    pass


def kernel(*refs):
    r = Refs()
    names = INPUTS + OUTPUTS + tuple(BUFFERS) + tuple(n + e for n in SEMS for e in ("_s", "_r"))
    for name, ref in zip(names, refs, strict=True):
        setattr(r, name, ref)

    def sems(name, *at):
        return getattr(r, name + "_s").at[at], getattr(r, name + "_r").at[at]

    dp, fr = lax.axis_index("dp"), lax.axis_index("frame")
    y, core, z, x = lax.div(dp, 2), lax.rem(dp, 2), lax.div(fr, NX), lax.rem(fr, NX)
    other, me = 1 - core, y * NX + x

    def device(yy, cc, zz, xx):
        return (yy * 2 + cc, zz * NX + xx)

    partner = device(y, other, z, x)

    def at_z(k):
        zz = lax.rem(z + k, NZ)
        return zz, device(y, core, zz, x)

    def at_x(k):
        xx = lax.rem(x + k, NX)
        return xx, device(y, core, z, xx)

    def at_y(k):
        yy = lax.rem(y + k, NY)
        return yy, device(yy, core, z, x)

    def at_plane(k):
        p = lax.rem(me + k, NP)
        return p, device(lax.div(p, NX), core, z, lax.rem(p, NX))

    def each(lo, hi, act):
        @pl.loop(lo, hi)
        def _(k):
            act(k)

    barrier = pltpu.get_barrier_semaphore()

    def greet(to):
        pl.semaphore_signal(barrier, inc=1, device_id=to, device_id_type=MESH)

    each(1, NZ, lambda k: greet(at_z(k)[1]))
    each(1, NP, lambda k: greet(at_plane(k)[1]))
    greet(partner)
    r.pair[core] = r.shard[core]
    r.gob[z] = r.grad[...]

    def norm_frames(i):
        @pl.loop(i * 2, i * 2 + 2)
        def _(b):
            span = pl.ds(pl.multiple_of(b * 32, 32), 32)
            hat, _ = norm_rows(r.frames[span, :].astype(F32))
            r.hat[span, :] = hat
            r.normed[span, :] = (hat * r.media_gain[...]).astype(BF16)

    def reorder(ref):
        for i in range(4):
            lanes = slice(i * 384, i * 384 + 384)
            ref[:, lanes] = dot(ref[:, lanes], r.order[...]).astype(BF16)

    pl.semaphore_wait(barrier, NZ - 1 + NP - 1 + 1)

    swap = push(r.shard.at[other], r.pair.at[core], *sems("swap", 0), partner)
    swap.start()

    def go(way, s):
        slot = lax.rem(z + (NZ + 1 - s if way == 0 else s - 1), NZ)
        to = at_z(1 if way == 0 else NZ - 1)[1]
        return push(r.gob.at[slot], r.gob.at[slot], *sems("go", way, s), to)

    def go_start(s):
        go(0, s).start()
        if s < 8:
            go(1, s).start()

    def go_next(s):
        go(0, s).wait_recv()
        if s < 8:
            go(1, s).wait_recv()
            go_start(s + 1)

    swap.wait()
    r.pair_rows[...] = jnp.zeros_like(r.pair_rows)
    r.pair_rows[0:3] = r.pair[0, 0:3].astype(F32)
    r.pair_rows[3:6] = r.pair[1, 0:3].astype(F32)
    r.zbuf[z] = r.pair_rows[...].astype(BF16)

    def along_z(k):
        return push(r.zbuf.at[z], r.zbuf.at[z], *sems("along_z", k), at_z(k)[1])

    each(1, NZ, lambda k: along_z(k).start())
    go_start(1)
    norm_frames(0)
    norm_frames(1)
    go_next(1)
    each(1, NZ, lambda k: along_z(k).wait_recv())
    for k in range(NZ):
        r.rows[6 * k : 6 * k + 6] = r.zbuf[k, 0:6].astype(F32)
    for u in range(2):
        r.wkv[core, u, y, x] = r.rows[:, u * 256 : u * 256 + 256].astype(BF16)
        r.wq[core, u, y, x] = r.rows[:, 512 + u * 128 : 640 + u * 128].astype(BF16)

    def second(ref, name, u, k):
        block = ref.at[core, u, y, x]
        return push(block, block, *sems(name, u, k), (at_y, at_x)[u](k)[1])

    def line(ref, u, turn):
        if u == 0:
            return ref.at[core, 0, :, lax.rem(x + turn, NX)]
        return ref.at[core, 1, lax.rem(y + turn, NY)]

    def third(ref, name, u, k):
        return push(line(ref, u, 0), line(ref, u, 0), *sems(name, u, k), (at_x, at_y)[u](k)[1])

    def fourth(ref, name, u, k):
        return push(line(ref, u, 4 - k), line(ref, u, 4 - k), *sems(name, u, k), partner)

    def for_all(act, *args):
        for k in (1, 3, 2):
            for u in range(2):
                act(*args, u, k)

    for_all(lambda u, k: second(r.wkv, "kv2", u, k).start())
    for_all(lambda u, k: second(r.wq, "q2", u, k).start())
    norm_frames(2)
    norm_frames(3)
    go_next(2)
    for_all(lambda u, k: second(r.wkv, "kv2", u, k).wait_recv())
    for_all(lambda u, k: third(r.wkv, "kv3", u, k).start())
    for u in range(2):
        fourth(r.wkv, "kv4", u, 0).start()
    go_next(3)
    reorder(r.normed)
    hat, lat_inverse = norm_rows(r.latents[...])
    r.lat_normed[...] = (hat * r.latent_gain[...]).astype(BF16)
    reorder(r.lat_normed)
    for_all(lambda u, k: second(r.wq, "q2", u, k).wait_recv())
    go_next(4)
    for k in (1, 3, 2):
        for u in range(2):
            third(r.wkv, "kv3", u, k).wait_recv()
            fourth(r.wkv, "kv4", u, k).start()
        if k != 2:
            go_next(5 + k // 2)
    for_all(lambda u, k: third(r.wq, "q3", u, k).start())
    for u in range(2):
        fourth(r.wq, "q4", u, 0).start()
    for k in (0, 1, 3, 2):
        for u in range(2):
            fourth(r.wkv, "kv4", u, k).wait_recv()

    def kv_proj(c, u):
        return r.wkv[c, u].reshape(WIDTH, 256)

    def q_proj(c, u):
        return r.wq[c, u].reshape(WIDTH, 128)

    for c in range(2):
        for u in range(2):
            lanes = slice(c * 512 + u * 256, c * 512 + u * 256 + 256)
            r.kv[:, lanes] = dot(r.normed[...], kv_proj(c, u)).astype(BF16)

    def slot_owner(slot):
        return ((slot >> 3) & (NZ - 1)) * NX + (slot >> 7)

    slot, lane = iota((NX * SLOTS, ROWS), 0), iota((NX * SLOTS, ROWS), 1)
    chosen = (r.route_lane[0:1] == slot_owner(slot)) & ((slot & 7) == (lane & 7))
    chosen = jnp.where(chosen, 1.0, 0.0)
    chosen_low = chosen.astype(BF16)
    alive = jnp.sum(chosen, axis=1, keepdims=True)

    def out_x(k):
        xx, to = at_x(k)
        return push(r.slots.at[xx], r.got.at[x], *sems("out_x", k), to)

    for i in range(NX):
        span = slice(i * SLOTS, i * SLOTS + SLOTS)
        r.slots[i, :, : 2 * INNER] = dot(chosen_low[span], r.kv[...]).astype(BF16)
        r.slots[i, :, 2 * INNER :] = jnp.broadcast_to(alive[span], (SLOTS, 128)).astype(BF16)
    for k in (1, 3, 2):
        out_x(k).start()
    r.got[x] = r.slots[x]
    go_next(7)
    for k in (1, 3, 2):
        for u in range(2):
            third(r.wq, "q3", u, k).wait_recv()
            fourth(r.wq, "q4", u, k).start()
    for k in (0, 1, 3, 2):
        for u in range(2):
            fourth(r.wq, "q4", u, k).wait_recv()
    query = jnp.concatenate([dot(r.lat_normed[...], q_proj(c, u)) for c in range(2) for u in range(2)], axis=1)
    r.qrow[...] = by_head((query * HEAD**-0.5).astype(BF16))
    for c in range(2):
        for u in range(2):
            lanes = slice(c * 512 + u * 256, c * 512 + u * 256 + 256)
            r.lat_kv[:, lanes] = dot(r.lat_normed[...], kv_proj(c, u)).astype(BF16)
    r.lat_scores[...] = dot_nt(r.lat_kv[:, :INNER], r.qrow[...])
    go_next(8)

    @pl.loop(0, NZ)
    def _(s):
        r.gorow[s] = by_head(r.gob[s])

    r.lat_gprob[...] = dot_nt(r.lat_kv[:, INNER:], r.gorow[z])
    for k in (1, 3, 2):
        out_x(k).wait_recv()

    got = r.got[...].reshape(NZ * KEYS, SEND)
    for i in range(4):
        span = slice(i * 128, i * 128 + 128)
        r.kvs[i * 4 : i * 4 + 4] = dot(r.sorting[span], got).astype(BF16).reshape(4, KEYS, SEND)
    r.scores[...] = dot_nt(r.kvs[:, :, :INNER].reshape(NZ * KEYS, INNER), r.qrow[...]).reshape(NZ, KEYS, INNER)

    @pl.loop(0, NZ)
    def _(s):
        live = jnp.concatenate([r.kvs[s, :, 2 * INNER :].astype(F32)] * 4, axis=1)
        scores = jnp.where(live > 0.5, r.scores[s], DEAD)
        gprob = dot_nt(r.kvs[s, :, INNER : 2 * INNER], r.gorow[s])
        top = jnp.max(scores, axis=0, keepdims=True)
        weight = jnp.exp(scores - top)
        r.scores[s] = scores
        r.gprob[s] = gprob
        r.stat[s, 0] = top
        r.stat[s, 1] = jnp.sum(weight, axis=0, keepdims=True)
        r.stat[s, 2] = jnp.sum(weight * gprob, axis=0, keepdims=True)

    def stat_to(k):
        zz, to = at_z(k)
        return push(r.stat.at[zz], r.stat_got.at[z], *sems("stat_to", k), to)

    each(1, NZ, lambda k: stat_to(k).start())
    r.stat_got[z] = r.stat[z]
    top = jnp.max(r.lat_scores[...], axis=0, keepdims=True)
    weight = jnp.exp(r.lat_scores[...] - top)
    total = jnp.sum(weight, axis=0, keepdims=True)
    mixed = jnp.sum(weight * r.lat_gprob[...], axis=0, keepdims=True)
    each(1, NZ, lambda k: stat_to(k).wait_recv())
    best = top
    for i in range(NZ):
        best = jnp.maximum(best, r.stat_got[i, 0])
    total = total * jnp.exp(top - best)
    mixed = mixed * jnp.exp(top - best)
    for i in range(NZ):
        factor = jnp.exp(r.stat_got[i, 0] - best)
        total = total + r.stat_got[i, 1] * factor
        mixed = mixed + r.stat_got[i, 2] * factor
    r.stat_own[0] = best
    r.stat_own[1] = 1.0 / total
    r.stat_own[2] = mixed / total

    def stat_from(k):
        return push(r.stat_own, r.stat_all.at[z], *sems("stat_from", k), at_z(k)[1])

    each(1, NZ, lambda k: stat_from(k).start())
    r.stat_all[z] = r.stat_own[...]

    prob = jnp.exp(r.lat_scores[...] - r.stat_own[0]) * r.stat_own[1]
    lat_low = prob.astype(BF16)
    lat_gs = (prob * (r.lat_gprob[...] - r.stat_own[2])).astype(BF16)
    r.lat_out[0] = head_blocks(lat_gs, r.lat_kv[:, :INNER])
    r.lat_out[1] = dot(lat_gs, r.qrow[...])
    r.lat_out[2] = dot(lat_low, r.gorow[z])
    r.lat_out[3] = head_blocks(lat_low, r.lat_kv[:, INNER:])
    each(1, NZ, lambda k: stat_from(k).wait_recv())

    @pl.loop(0, NZ)
    def _(s):
        prob = jnp.exp(r.scores[s] - r.stat_all[s, 0]) * r.stat_all[s, 1]
        low = prob.astype(BF16)
        r.gs[s] = (prob * (r.gprob[s] - r.stat_all[s, 2])).astype(BF16)
        r.gkv[s, :, INNER:] = dot(low, r.gorow[s]).astype(BF16)
        r.part[s] = head_blocks(low, r.kvs[s, :, INNER : 2 * INNER])

    gs = r.gs[...].reshape(NZ * KEYS, INNER)
    r.gkv[:, :, :INNER] = dot(gs, r.qrow[...]).astype(BF16).reshape(NZ, KEYS, INNER)
    gkv = r.gkv[...].reshape(NZ * KEYS, 2 * INNER)

    def back_x(k):
        xx, to = at_x(k)
        return push(r.back.at[xx], r.back_got.at[x], *sems("back_x", k), to)

    for i in range(NX):
        span = slice(i * SLOTS, i * SLOTS + SLOTS)
        r.back[i] = dot_tn(r.sorting[:, span], gkv).astype(BF16)
    for k in (1, 3, 2):
        back_x(k).start()

    def ring(way, s):
        to = at_z(1 if way == 0 else NZ - 1)[1]
        return push(r.ring_out.at[way, s], r.ring_in.at[way, s], *sems("ring", way, s), to)

    def ring_send(s):
        for way in range(2 if s < 8 else 1):
            owner = lax.rem(z + (9 - s if way == 0 else 8 + s), NZ)
            value = r.part[owner]
            if s > 1:
                value = value + r.ring_in[way, s - 1].astype(F32)
            r.ring_out[way, s] = value.astype(BF16)
            ring(way, s).start()

    def ring_wait(s):
        for way in range(2 if s < 8 else 1):
            ring(way, s).wait_recv()

    def ring_next(s):
        ring_wait(s)
        ring_send(s + 1)

    ring_send(1)
    gquery = (head_blocks(gs, r.kvs[:, :, :INNER].reshape(NZ * KEYS, INNER)) + r.lat_out[0]) * HEAD**-0.5
    own = jnp.concatenate([gquery, r.lat_out[1], r.lat_out[2]], axis=1)
    for c in range(2):
        for p in range(NP):
            for j in range(3):
                first = c * 768 + p % 2 * 384 + j * 128
                r.sums[c, p, j] = own[p // 2 * 8 : p // 2 * 8 + 8, first : first + 128]
    sum_core = push(r.sums.at[other], r.sums_core, *sems("sum_core", 0), partner)
    sum_core.start()
    ring_next(1)
    sum_core.wait_recv()

    @pl.loop(0, NP)
    def _(p):
        r.sums_core[p] = r.sums_core[p] + r.sums[core, p]

    def sum_plane(k):
        p, to = at_plane(k)
        return push(r.sums_core.at[p], r.sums_plane.at[me], *sems("sum_plane", k), to)

    each(1, NP, lambda k: sum_plane(k).start())
    r.sums_plane[me] = r.sums_core[me]
    ring_next(2)
    for k in (1, 3, 2):
        back_x(k).wait_recv()
    r.back_got[x] = r.back[x]
    ring_next(3)

    slot = iota((ROWS, NX * SLOTS), 1)
    route = jnp.concatenate([r.route_rows[...]] * 4, axis=1)
    mine = (route == slot_owner(slot)) & ((slot & 7) == (iota((ROWS, NX * SLOTS), 0) & 7))
    mine = jnp.where(mine, 1.0, 0.0).astype(BF16)
    r.kv[...] = dot(mine, r.back_got[...].reshape(NX * SLOTS, 2 * INNER)).astype(BF16)
    grad_norm = 0.0
    for c in range(2):
        for u in range(2):
            lanes = slice(c * 512 + u * 256, c * 512 + u * 256 + 256)
            grad_norm = grad_norm + dot_nt(r.kv[:, lanes], kv_proj(c, u))
    r.normed[...] = grad_norm.astype(BF16)
    for i in range(4):
        lanes = slice(i * 384, i * 384 + 384)
        natural = dot_nt(r.normed[:, lanes], r.order[...])
        term = jnp.sum(natural * r.hat[:, lanes], axis=0, keepdims=True)
        for j in range(3):
            r.media[i * 3 + j] = term[:, j * 128 : j * 128 + 128]
    for i in range(12, NP):
        r.media[i] = jnp.zeros((1, 128), F32)
    med_core = push(r.media, r.media_core, *sems("med_core", 0), partner)
    med_core.start()
    each(1, NP, lambda k: sum_plane(k).wait_recv())
    ring_next(4)
    partial = r.sums_plane[0]
    for p in range(1, NP):
        partial = partial + r.sums_plane[p]
    r.chunk[0:3] = partial
    med_core.wait_recv()

    @pl.loop(0, NP)
    def _(p):
        r.media_core[p] = r.media_core[p] + r.media[p]

    def med_plane(k):
        p, to = at_plane(k)
        return push(r.media_core.at[p], r.media_plane.at[me], *sems("med_plane", k), to)

    each(1, NP, lambda k: med_plane(k).start())
    r.media_plane[me] = r.media_core[me]

    def red_z(j):
        return push(r.chunk.at[j], r.chunk_got.at[j, z], *sems("red_z", j, z), device(y, core, 4 * j, x))

    def red_z_in(j, k):
        sender = lax.rem(4 * j + k, NZ)
        return push(r.chunk.at[j], r.chunk_got.at[j, sender], *sems("red_z", j, sender), device(y, core, 4 * j, x))

    def reduce_start(j):
        @pl.when(z != 4 * j)
        def _():
            red_z(j).start()

        @pl.when(z == 4 * j)
        def _():
            r.chunk_got[j, 4 * j] = r.chunk[j]

    def all_z(j, k):
        tile = r.whole.at[core, me, j]
        return push(tile, tile, *sems("all_z", j, k), device(y, core, lax.rem(4 * j + k, NZ), x))

    def all_z_in(j):
        k = lax.rem(z + NZ - 4 * j, NZ)
        tile = r.whole.at[core, me, j]
        return push(tile, tile, *sems("all_z", j, k), device(y, core, lax.rem(4 * j + 1, NZ), x))

    def reduce_end(j):
        @pl.when(z == 4 * j)
        def _():
            each(1, NZ, lambda k: red_z_in(j, k).wait_recv())
            value = r.chunk_got[j, 0]
            for i in range(1, NZ):
                value = value + r.chunk_got[j, i]
            r.whole[core, me, j] = value
            each(1, NZ, lambda k: all_z(j, k).start())

    for j in range(3):
        reduce_start(j)
    each(1, NP, lambda k: med_plane(k).wait_recv())
    partial = r.media_plane[0]
    for p in range(1, NP):
        partial = partial + r.media_plane[p]
    r.chunk[3] = jnp.broadcast_to(partial, (8, 128))
    reduce_start(3)
    ring_next(5)
    for j in range(4):
        reduce_end(j)
    ring_next(6)
    for j in range(4):
        @pl.when(z != 4 * j)
        def _():
            all_z_in(j).wait_recv()

    def all_plane(k):
        block = r.whole.at[core, me]
        return push(block, block, *sems("all_plane", k), at_plane(k)[1])

    def all_core(p):
        block = r.whole.at[core, p]
        return push(block, block, *sems("all_core", p), partner)

    each(1, NP, lambda k: all_plane(k).start())
    all_core(me).start()
    ring_next(7)

    def forward(k):
        all_plane(k).wait_recv()
        all_core(lax.rem(me + NP - k, NP)).start()

    each(1, NP, forward)
    ring_wait(8)
    r.attended[...] = (
        r.part[z] + r.lat_out[3] + r.ring_in[0, 8].astype(F32) + r.ring_in[1, 7].astype(F32)
    ).astype(BF16)
    each(0, NP, lambda p: all_core(p).wait_recv())

    def gathered(c, rows, g, j):
        return r.whole[c, rows * 2 + g, j]

    strips = []
    for c in range(2):
        for g in range(2):
            for j in range(3):
                strips.append(jnp.concatenate([gathered(c, rows, g, j) for rows in range(8)], axis=0))

    def precise(values, weight):
        high = values.astype(BF16)
        low = (values - high.astype(F32)).astype(BF16)
        result = dot_nt(jnp.concatenate([high, low], axis=0), weight)
        return result[:LAT] + result[LAT:]

    grad = 0.0
    for i in range(4):
        grad = grad + precise(strips[i], q_proj(i // 2, i % 2))
        both = jnp.concatenate([strips[4 + 2 * i], strips[5 + 2 * i]], axis=1)
        grad = grad + precise(both, kv_proj(i // 2, i % 2))
    natural = []
    for i in range(4):
        rest = grad[:, i * 384 : i * 384 + 384]
        pieces = []
        for _ in range(3):
            piece = rest.astype(BF16)
            rest = rest - piece.astype(F32)
            pieces.append(piece)
        moved = dot_nt(jnp.concatenate(pieces, axis=0), r.order[...])
        natural.append(moved[:LAT] + moved[LAT : 2 * LAT] + moved[2 * LAT :])
    grad = jnp.concatenate(natural, axis=1)
    hat, lat_inverse = norm_rows(r.latents[...])
    r.latent_gain_grad[...] = jnp.sum(grad * hat, axis=0, keepdims=True)
    grad_hat = grad * r.latent_gain[...]
    r.latent_grad[...] = lat_inverse * (
        grad_hat
        - jnp.mean(grad_hat, -1, keepdims=True)
        - hat * jnp.mean(grad_hat * hat, -1, keepdims=True)
    )
    for p in range(12):
        r.media_gain_grad[:, p * 128 : p * 128 + 128] = r.whole[core, p, 3][0:1]

    each(1, NZ, lambda k: along_z(k).wait_send())
    for s in range(1, 9):
        for way in range(2 if s < 8 else 1):
            go(way, s).wait_send()
            ring(way, s).wait_send()
    for ref, name in ((r.wkv, "kv"), (r.wq, "q")):
        for u in range(2):
            for k in range(4):
                if k:
                    second(ref, name + "2", u, k).wait_send()
                    third(ref, name + "3", u, k).wait_send()
                fourth(ref, name + "4", u, k).wait_send()
    for k in range(1, 4):
        out_x(k).wait_send()
        back_x(k).wait_send()
    each(1, NZ, lambda k: stat_to(k).wait_send())
    each(1, NZ, lambda k: stat_from(k).wait_send())
    sum_core.wait_send()
    med_core.wait_send()
    each(1, NP, lambda k: sum_plane(k).wait_send())
    each(1, NP, lambda k: med_plane(k).wait_send())
    for j in range(4):
        @pl.when(z != 4 * j)
        def _():
            red_z(j).wait_send()

        @pl.when(z == 4 * j)
        def _():
            each(1, NZ, lambda k: all_z(j, k).wait_send())
    each(1, NP, lambda k: all_plane(k).wait_send())
    each(0, NP, lambda p: all_core(p).wait_send())


def body(frame_features, frame_owner, latents, latent_gain, media_gain, query_proj, keyval_proj, grad_output):
    half = INNER // 2
    shard = jnp.stack(
        [
            jnp.concatenate([keyval_proj[:, :INNER], query_proj[:, :half]], axis=1),
            jnp.concatenate([keyval_proj[:, INNER:], query_proj[:, half:]], axis=1),
        ]
    )
    shard = jnp.pad(shard, ((0, 0), (0, 5), (0, 0)))
    route = jnp.repeat(frame_owner[0, :, 0], TOK)
    scratch = [pltpu.VMEM(*spec) for spec in BUFFERS.values()]
    scratch += [DMA(shape) for shape in SEMS.values() for _ in range(2)]
    vmem = pl.BlockSpec(memory_space=pltpu.VMEM)
    attended, latent_grad, latent_gain_grad, media_gain_grad = pl.pallas_call(
        kernel,
        out_shape=(
            jax.ShapeDtypeStruct((LAT, INNER), BF16),
            jax.ShapeDtypeStruct((LAT, WIDTH), F32),
            jax.ShapeDtypeStruct((1, WIDTH), F32),
            jax.ShapeDtypeStruct((1, WIDTH), F32),
        ),
        in_specs=[vmem] * len(INPUTS),
        out_specs=(vmem,) * 4,
        scratch_shapes=scratch,
        compiler_params=pltpu.CompilerParams(collective_id=0, has_side_effects=True, vmem_limit_bytes=60 << 20),
        name="resampler",
    )(
        shard,
        frame_features.reshape(ROWS, WIDTH),
        latents,
        latent_gain.reshape(1, WIDTH),
        media_gain.reshape(1, WIDTH),
        jnp.broadcast_to(route[None, :], (8, ROWS)),
        jnp.broadcast_to(route[:, None], (ROWS, 128)),
        grad_output[0, 0],
        jnp.asarray(gathered_order(), BF16),
        jnp.asarray(sample_order(), BF16),
    )
    return (attended[None, None], latent_grad, latent_gain_grad[0], media_gain_grad[0])


def solution(mesh):
    placed = (
        P("dp", "frame", None, None),
        P("dp", "frame", None),
        P(),
        P(),
        P(),
        P(("dp", "frame"), None),
        P(("dp", "frame"), None),
        P("dp", "frame", None, None),
    )
    return jax.shard_map(
        body,
        mesh=mesh,
        in_specs=placed,
        out_specs=(P("dp", "frame", None, None), P(), P(), P()),
        check_vma=False,
    )
```

time: 1080 us -> 163 us (0.15)
  waiting for transfers between devices: 852 us -> 0 us
  Pallas kernels: 0 us -> 152 us
  blocking collectives: 105 us -> 0 us
  starting transfers between devices: 38.8 us -> 0 us
  matrix products: 28.6 us -> 0 us
  local copies, waits for them, and re-layouts: 29.7 us -> 8.29 us
  between operations: 14.1 us -> 0.68 us
    psum x1 -> x0, waiting for transfers between devices: 481 us -> none  [body(): lax.psum((grad_query * score_scale, grad_keyval[media_rows:], media_term)...]
    all_gather x2 -> x0, waiting for transfers between devices: 364 us -> none  [the longest x1 193 us: body(): lax.all_gather(keyval_proj, ('dp', 'frame'), axis=0, tiled=True)]
    pallas_call x0 -> x1, Pallas kernels: none -> 152 us  [body(): pl.pallas_call(kernel, out_shape=(jax.ShapeDtypeStruct((LAT, INNER), BF16...]
    psum x1 -> x0, blocking collectives: 105 us -> none  [body(): lax.psum((grad_query * score_scale, grad_keyval[media_rows:], media_term)...]
    all_to_all x3 -> x0, starting transfers between devices: 38.5 us -> none  [the longest x1 19.1 us: body(): lax.all_to_all(slot_live, 'frame', split_axis=0, concat_axis=0, tiled=True)]
    dot_general x15 -> x0, matrix products: 25.9 us -> none  [the longest x2 3.3 us: precise_times(): lax.dot_general(upper, weight, dims, preferred_element_type=jnp.float32)]
    unnamed x60 -> x14, local copies, waits for them, and re-layouts: 22.1 us -> 4.86 us
  transfers between devices with their start and end apart: 6 -> 0, of which waited for: 4 -> 0; matrix products, arithmetic and copies ran while one was open for 4% -> 0% of each run, Pallas kernels for 0% -> 0%
where the time goes in v2:
time: 163 us
  Pallas kernels  152 us (93%)
  local copies, waits for them, and re-layouts  8.29 us (5%)
  other arithmetic  1.87 us (1%)
    pallas_call x1, Pallas kernels, body(): pl.pallas_call(kernel, out_shape=(jax.ShapeDtypeStruct((LAT, INNER), BF16...  152 us
    unnamed x14, local copies, waits for them, and re-layouts  4.86 us

profile of v2, /device:TPU:1, one launch (start us, length us, event | category | flops | bytes accessed | tf_op | source)
XLA Modules:
  0.0 162.7 jit_solution(9366386787625066276)
XLA Ops:
  0.6 0.0 copy-start.4
  0.6 0.7 fusion.3
  1.4 0.0 copy-done.4
  1.4 0.6 fusion.2.refs_0_
  2.0 0.0 copy-start.5
  2.0 0.7 copy-done.5
  2.7 0.1 broadcast_in_dim.18
  2.7 0.1 broadcast_in_dim.19
  2.8 0.8 broadcast_in_dim.21.refs_6_
  3.6 0.0 copy-start
  3.6 0.6 broadcast_in_dim.20.refs_5_
  4.2 0.1 copy-done
  4.3 0.0 copy-start.1
  4.3 0.6 reshape.20.refs_3_
  4.9 0.1 copy-done.1
  5.0 0.6 reshape.21.refs_4_
  5.6 151.9 %resampler.1 = (bf16[64,512]{1,0:T(8,128)(2,1)}, f32[64,1536]{1,0:T(8,128)}, f32[1,1536]{1,0:T(1,128)}, f32[1,1536]{1,0:T(1,128)}) custom-call(bf16[2,8,768]{2,1,0:T(8,128)(2,1)} %fusion.2.refs_0_, bf16[256,1536]{1,0:T(8,128)(2,1)} %bitcast.8, f32[64,1536]{1,0:T(8,128)} %refs_2_.1, f32[1,1536]{1,0:T(1,128)} %reshape.20.refs_3_, f32[1,1536]{1,0:T(1,128)} %reshape.21.refs_4_, ...), custom_call_target="tpu_custom_call" | custom-call | tf_op jit(solution)/shard_map/resampler/pallas_call | solution.py:678
  157.5 0.0 copy-start.3
  157.5 0.7 copy-done.3
  158.2 0.0 copy-start.2
  158.2 0.6 reduce
  158.8 0.1 copy-done.2
  158.9 0.6 reduce.1
  159.5 1.5 copy.16
  161.0 1.8 %copy.17 = f32[64,1536]{1,0:T(8,128)} copy(f32[64,1536]{1,0:T(8,128)} %get-tuple-element.23) | data formatting | bytes 786432
  (2 shorter events, 0.0 us)
Async XLA Ops:
  0.6 0.7 copy-start.4
  2.0 0.7 copy-start.5
  3.6 0.7 copy-start
  4.3 0.7 copy-start.1
  157.5 0.7 copy-start.3
  158.2 0.7 copy-start.2

commit v3 on v2

v3 whole, which is shorter than its diff:
```python
import jax
import jax.numpy as jnp
from jax import lax
from jax.experimental import pallas as pl
from jax.experimental.pallas import tpu as pltpu
from jax.sharding import PartitionSpec as P

NX, NY, NZ = 4, 4, 16
NP = NX * NY
HEADS, HEAD, INNER, WIDTH, LAT = 8, 64, 512, 1536, 64
TOK, FRAMES = 8, 32
ROWS = FRAMES * TOK
KEYS = NX * TOK
SLOTS = NZ * TOK
SEND = 2 * INNER + 128
DEAD = -1e30
MESH = pl.DeviceIdType.MESH
F32, BF16 = jnp.float32, jnp.bfloat16
DMA = pltpu.SemaphoreType.DMA


def dot(left, right, dims=((1,), (0,))):
    return lax.dot_general(left, right, (dims, ((), ())), preferred_element_type=F32)


def dot_nt(left, right):
    return dot(left, right, ((1,), (1,)))


def dot_tn(left, right):
    return dot(left, right, ((0,), (0,)))


def norm_rows(values):
    center = values - jnp.mean(values, -1, keepdims=True)
    inverse = lax.rsqrt(jnp.mean(center * center, -1, keepdims=True) + 1e-05)
    return center * inverse, inverse


def iota(shape, dim):
    return lax.broadcasted_iota(jnp.int32, shape, dim)


def gathered_order():
    place = iota((384, 384), 1)
    block = (place >= 96).astype(jnp.int32) + (place >= 192).astype(jnp.int32) + (place >= 288).astype(jnp.int32)
    inner = place - block * 96
    six = (inner * 43) >> 8
    last = inner - six * 6
    odd = (last >= 3).astype(jnp.int32)
    natural = odd * 192 + six * 12 + block * 3 + last - odd * 3
    return jnp.where(iota((384, 384), 0) == natural, 1.0, 0.0).astype(BF16)


def sample_order():
    shape = (NZ * KEYS, NZ * KEYS)
    place = iota(shape, 0)
    source = (((place >> 3) & 3) << 7) + ((place >> 5) << 3) + (place & 7)
    return jnp.where(iota(shape, 1) == source, 1.0, 0.0).astype(BF16)


def source_order():
    shape = (NZ * KEYS, NZ * KEYS)
    place = iota(shape, 0)
    sample = (((place >> 3) & (NZ - 1)) << 5) + ((place >> 7) << 3) + (place & 7)
    return jnp.where(iota(shape, 1) == sample, 1.0, 0.0).astype(BF16)


def by_head(ref, rows):
    for head in range(HEADS):
        lanes = slice(head // 2 * 128, head // 2 * 128 + 128)
        own = (iota((LAT, 128), 1) >> 6) == head % 2
        part = jnp.where(own, rows[:, lanes].astype(F32), 0.0).astype(BF16)
        ref[head * LAT : head * LAT + LAT, lanes] = part


def head_blocks(left, right):
    blocks = []
    for pair in range(HEADS // 2):
        lanes = slice(pair * 128, pair * 128 + 128)
        both = dot_tn(left[:, lanes], right[:, lanes])
        blocks.append(jnp.where(iota((HEAD, 128), 1) < HEAD, both[:HEAD], both[HEAD:]))
    return jnp.concatenate(blocks, axis=1)


def push(src, dst, send, recv, to):
    return pltpu.make_async_remote_copy(
        src_ref=src, dst_ref=dst, send_sem=send, recv_sem=recv, device_id=to, device_id_type=MESH
    )


INPUTS = ("keyval", "query", "frames", "latents", "latent_gain", "media_gain", "route", "grad")
OUTPUTS = ("attended", "latent_grad", "lat_inverse", "latent_gain_grad", "media_gain_grad")
BUFFERS = dict(
    order=((384, 384), BF16),
    sorting=((NZ * KEYS, NZ * KEYS), BF16),
    resorting=((NZ * KEYS, NZ * KEYS), BF16),
    low=((NZ, KEYS, INNER), BF16),
    shard=((2, 8, 768), BF16),
    pair=((2, 8, 768), BF16),
    pair_rows=((8, 768), F32),
    zkv=((NZ, 8, 512), BF16),
    zq=((NZ, 8, 256), BF16),
    rows=((6 * NZ, 768), F32),
    wkv=((2, 2, NY, NX, 6 * NZ, 256), BF16),
    wq=((2, 2, NY, NX, 6 * NZ, 128), BF16),
    gob=((NZ, LAT, INNER), BF16),
    hat=((ROWS, WIDTH), F32),
    normed=((ROWS, WIDTH), BF16),
    kv=((ROWS, SEND), BF16),
    mine=((ROWS, NX * SLOTS), BF16),
    slots=((NX, SLOTS, SEND), BF16),
    got=((NX, SLOTS, SEND), BF16),
    kvs=((NZ, KEYS, SEND), BF16),
    lat_normed=((LAT, WIDTH), BF16),
    lat_kv=((LAT, 2 * INNER), BF16),
    qrow=((HEADS * LAT, INNER), BF16),
    gorow=((NZ, HEADS * LAT, INNER), BF16),
    scores=((NZ, KEYS, INNER), F32),
    gprob=((NZ, KEYS, INNER), F32),
    lat_scores=((LAT, INNER), F32),
    lat_gprob=((LAT, INNER), F32),
    stat=((NZ, 2, 1, INNER), F32),
    stat_got=((NZ, 2, 1, INNER), F32),
    stat_own=((2, 1, INNER), F32),
    stat_all=((NZ, 2, 1, INNER), F32),
    gs=((NZ, KEYS, INNER), BF16),
    gkv=((NZ, KEYS, 2 * INNER), BF16),
    back=((NX, SLOTS, 2 * INNER), BF16),
    back_got=((NX, SLOTS, 2 * INNER), BF16),
    lat_out=((4, LAT, INNER), F32),
    part=((4, 4, LAT, INNER), BF16),
    near_in=((3, 4, LAT, INNER), BF16),
    far_out=((4, LAT, INNER), BF16),
    far_in=((4, LAT, INNER), BF16),
    own_part=((LAT, INNER), F32),
    sums=((2, NP, 3, 8, 128), F32),
    sums_core=((NP, 3, 8, 128), F32),
    sums_plane=((NP, 3, 8, 128), F32),
    chunk=((3, 8, 128), F32),
    sum_quads=((4, 3, 8, 128), F32),
    sum_class=((4, 3, 8, 128), F32),
    whole=((2, NP, 3, 8, 128), F32),
    media=((12, 1, 128), F32),
    media_core=((12, 1, 128), F32),
    med_quads=((4, 12, 1, 128), F32),
    med_class=((4, 12, 1, 128), F32),
    med_whole=((NP, 12, 1, 128), F32),
)
SEMS = dict(
    swap=(1,), along_z=(NZ,), along_q=(NZ,), go_far=(4,), go_near=(4, 3), kv2=(2, 4), kv3=(2, 4), kv4=(2, 4), q2=(2, 4), q3=(2, 4), q4=(2, 4),
    out_x=(4,), back_x=(4,), stat_to=(NZ,), stat_from=(NZ,), near=(3,), far=(4,), sum_core=(1,), sum_plane=(NP,),
    med_core=(1,), sum_far=(4,), sum_near=(3,), med_far=(4,), med_near=(3,), all_plane=(NP,), all_core=(NP,), med_all=(NP,),
)
NEAR = (1, NZ - 1, 2)


class Refs:
    pass


def kernel(*refs):
    r = Refs()
    names = INPUTS + OUTPUTS + tuple(BUFFERS) + tuple(n + e for n in SEMS for e in ("_s", "_r"))
    for name, ref in zip(names, refs, strict=True):
        setattr(r, name, ref)

    def sems(name, *at):
        return getattr(r, name + "_s").at[at], getattr(r, name + "_r").at[at]

    dp, fr = lax.axis_index("dp"), lax.axis_index("frame")
    y, core, z, x = lax.div(dp, 2), lax.rem(dp, 2), lax.div(fr, NX), lax.rem(fr, NX)
    other, me = 1 - core, y * NX + x

    def device(yy, cc, zz, xx):
        return (yy * 2 + cc, zz * NX + xx)

    partner = device(y, other, z, x)

    def at_z(k):
        zz = lax.rem(z + k, NZ)
        return zz, device(y, core, zz, x)

    def at_x(k):
        xx = lax.rem(x + k, NX)
        return xx, device(y, core, z, xx)

    def at_y(k):
        yy = lax.rem(y + k, NY)
        return yy, device(yy, core, z, x)

    def at_plane(k):
        p = lax.rem(me + k, NP)
        return p, device(lax.div(p, NX), core, z, lax.rem(p, NX))

    def each(lo, hi, act):
        @pl.loop(lo, hi)
        def _(k):
            act(k)

    barrier = pltpu.get_barrier_semaphore()

    def greet(to):
        pl.semaphore_signal(barrier, inc=1, device_id=to, device_id_type=MESH)

    each(1, NZ, lambda k: greet(at_z(k)[1]))
    each(1, NP, lambda k: greet(at_plane(k)[1]))
    greet(partner)
    r.gob[z] = r.grad[...]
    r.pair_rows[...] = jnp.zeros_like(r.pair_rows)
    for c in range(2):
        r.pair_rows[0:3, 0:512] = r.keyval[:, c * 512 : c * 512 + 512].astype(F32)
        r.pair_rows[0:3, 512:768] = r.query[:, c * 256 : c * 256 + 256].astype(F32)
        r.shard[c] = r.pair_rows[...].astype(BF16)
    r.pair[core] = r.shard[core]
    media_gain = r.media_gain[...].reshape(1, WIDTH)
    latent_gain = r.latent_gain[...].reshape(1, WIDTH)

    @pl.loop(0, ROWS // 32)
    def _(b):
        span = pl.ds(pl.multiple_of(b * 32, 32), 32)
        hat, _ = norm_rows(r.frames[span, :].astype(F32))
        r.hat[span, :] = hat
        r.normed[span, :] = (hat * media_gain).astype(BF16)

    def reorder(ref):
        for i in range(4):
            lanes = slice(i * 384, i * 384 + 384)
            ref[:, lanes] = dot(ref[:, lanes], r.order[...]).astype(BF16)

    r.order[...] = gathered_order()
    r.sorting[...] = sample_order()
    r.resorting[...] = source_order()
    r.qrow[...] = jnp.zeros_like(r.qrow)

    @pl.loop(0, NZ)
    def _(s):
        r.gorow[s] = jnp.zeros((HEADS * LAT, INNER), BF16)

    reorder(r.normed)
    hat, _ = norm_rows(r.latents[...])
    r.lat_normed[...] = (hat * latent_gain).astype(BF16)
    reorder(r.lat_normed)
    def slot_owner(slot):
        return ((slot >> 3) & (NZ - 1)) * NX + (slot >> 7)

    slot = iota((ROWS, NX * SLOTS), 1)
    route = jnp.concatenate([r.route[...]] * 4, axis=1)
    mine = (route == slot_owner(slot)) & ((slot & 7) == (iota((ROWS, NX * SLOTS), 0) & 7))
    r.mine[...] = jnp.where(mine, 1.0, 0.0).astype(BF16)
    r.kv[:, 2 * INNER :] = jnp.ones((ROWS, 128), BF16)
    pl.semaphore_wait(barrier, NZ - 1 + NP - 1 + 1)

    swap = push(r.shard.at[other], r.pair.at[core], *sems("swap", 0), partner)
    swap.start()

    def go_far(j):
        return push(r.gob.at[z], r.gob.at[z], *sems("go_far", j), at_z(4 * j)[1])

    def go_near(i, d):
        block = r.gob.at[lax.rem(z + 4 * i, NZ)]
        return push(block, block, *sems("go_near", i, d), at_z(NEAR[d])[1])

    swap.wait()
    r.pair_rows[...] = jnp.zeros_like(r.pair_rows)
    r.pair_rows[0:3] = r.pair[0, 0:3].astype(F32)
    r.pair_rows[3:6] = r.pair[1, 0:3].astype(F32)
    r.zkv[z] = r.pair_rows[:, :512].astype(BF16)
    r.zq[z] = r.pair_rows[:, 512:].astype(BF16)

    def along_z(k):
        return push(r.zkv.at[z], r.zkv.at[z], *sems("along_z", k), at_z(k)[1])

    def along_q(k):
        return push(r.zq.at[z], r.zq.at[z], *sems("along_q", k), at_z(k)[1])

    each(1, NZ, lambda k: along_z(k).start())
    each(1, NZ, lambda k: along_q(k).start())
    each(1, NZ, lambda k: along_z(k).wait_recv())
    for k in range(NZ):
        r.rows[6 * k : 6 * k + 6, :512] = r.zkv[k, 0:6].astype(F32)
    for u in range(2):
        r.wkv[core, u, y, x] = r.rows[:, u * 256 : u * 256 + 256].astype(BF16)

    def second(ref, name, u, k):
        block = ref.at[core, u, y, x]
        return push(block, block, *sems(name, u, k), (at_y, at_x)[u](k)[1])

    def line(ref, u, turn):
        if u == 0:
            return ref.at[core, 0, :, lax.rem(x + turn, NX)]
        return ref.at[core, 1, lax.rem(y + turn, NY)]

    def third(ref, name, u, k):
        return push(line(ref, u, 0), line(ref, u, 0), *sems(name, u, k), (at_x, at_y)[u](k)[1])

    def fourth(ref, name, u, k):
        return push(line(ref, u, 4 - k), line(ref, u, 4 - k), *sems(name, u, k), partner)

    def for_all(act, *args):
        for k in (1, 3, 2):
            for u in range(2):
                act(*args, u, k)

    for_all(lambda u, k: second(r.wkv, "kv2", u, k).start())
    each(1, NZ, lambda k: along_q(k).wait_recv())
    for k in range(NZ):
        r.rows[6 * k : 6 * k + 6, 512:] = r.zq[k, 0:6].astype(F32)
    for u in range(2):
        r.wq[core, u, y, x] = r.rows[:, 512 + u * 128 : 640 + u * 128].astype(BF16)
    for_all(lambda u, k: second(r.wq, "q2", u, k).start())
    for j in (2, 1, 3):
        go_far(j).start()
    for d in range(3):
        go_near(0, d).start()
    for_all(lambda u, k: second(r.wkv, "kv2", u, k).wait_recv())
    for_all(lambda u, k: third(r.wkv, "kv3", u, k).start())
    for u in range(2):
        fourth(r.wkv, "kv4", u, 0).start()
    for_all(lambda u, k: second(r.wq, "q2", u, k).wait_recv())
    for k in (1, 3, 2):
        for u in range(2):
            third(r.wkv, "kv3", u, k).wait_recv()
            fourth(r.wkv, "kv4", u, k).start()
    for_all(lambda u, k: third(r.wq, "q3", u, k).start())
    for u in range(2):
        fourth(r.wq, "q4", u, 0).start()
    for j in (1, 3, 2):
        go_far(j).wait_recv()
        for d in range(3):
            go_near(4 - j, d).start()
    for k in (0, 1, 3, 2):
        for u in range(2):
            fourth(r.wkv, "kv4", u, k).wait_recv()

    def kv_proj(c, u):
        return r.wkv[c, u].reshape(WIDTH, 256)

    def q_proj(c, u):
        return r.wq[c, u].reshape(WIDTH, 128)

    for c in range(2):
        for u in range(2):
            lanes = slice(c * 512 + u * 256, c * 512 + u * 256 + 256)
            r.kv[:, lanes] = dot(r.normed[...], kv_proj(c, u)).astype(BF16)

    def out_x(k):
        xx, to = at_x(k)
        return push(r.slots.at[xx], r.got.at[x], *sems("out_x", k), to)

    for i in range(NX):
        span = slice(i * SLOTS, i * SLOTS + SLOTS)
        r.slots[i] = dot_tn(r.mine[:, span], r.kv[...]).astype(BF16)
    for k in (1, 3, 2):
        out_x(k).start()
    r.got[x] = r.slots[x]
    for k in (1, 3, 2):
        for u in range(2):
            third(r.wq, "q3", u, k).wait_recv()
            fourth(r.wq, "q4", u, k).start()
    for k in (0, 1, 3, 2):
        for u in range(2):
            fourth(r.wq, "q4", u, k).wait_recv()
    query = jnp.concatenate([dot(r.lat_normed[...], q_proj(c, u)) for c in range(2) for u in range(2)], axis=1)
    by_head(r.qrow, (query * HEAD**-0.5).astype(BF16))
    for c in range(2):
        for u in range(2):
            lanes = slice(c * 512 + u * 256, c * 512 + u * 256 + 256)
            r.lat_kv[:, lanes] = dot(r.lat_normed[...], kv_proj(c, u)).astype(BF16)
    r.lat_scores[...] = dot_nt(r.lat_kv[:, :INNER], r.qrow[...])
    for i in range(4):
        for d in range(3):
            go_near(i, d).wait_recv()

    @pl.loop(0, NZ, unroll=2)
    def _(s):
        by_head(r.gorow.at[s], r.gob[s])

    r.lat_gprob[...] = dot_nt(r.lat_kv[:, INNER:], r.gorow[z])
    for k in (1, 3, 2):
        out_x(k).wait_recv()

    got = r.got[...].reshape(NZ * KEYS, SEND)
    for i in range(4):
        span = slice(i * 128, i * 128 + 128)
        r.kvs[i * 4 : i * 4 + 4] = dot(r.sorting[span], got).astype(BF16).reshape(4, KEYS, SEND)
    r.scores[...] = dot_nt(r.kvs[:, :, :INNER].reshape(NZ * KEYS, INNER), r.qrow[...]).reshape(NZ, KEYS, INNER)

    @pl.loop(0, NZ, unroll=4)
    def _(s):
        live = jnp.concatenate([r.kvs[s, :, 2 * INNER :].astype(F32)] * 4, axis=1)
        scores = jnp.where(live > 0.5, r.scores[s], DEAD)
        gprob = dot_nt(r.kvs[s, :, INNER : 2 * INNER], r.gorow[s])
        top = jnp.max(scores, axis=0, keepdims=True)
        weight = jnp.exp(scores - top)
        r.scores[s] = scores
        r.gprob[s] = gprob
        total = jnp.sum(weight, axis=0, keepdims=True)
        r.stat[s, 0] = top + jnp.log(total)
        r.stat[s, 1] = jnp.sum(weight * gprob, axis=0, keepdims=True) / total

    def stat_to(k):
        zz, to = at_z(k)
        return push(r.stat.at[zz], r.stat_got.at[z], *sems("stat_to", k), to)

    each(1, NZ, lambda k: stat_to(k).start())
    r.stat_got[z] = r.stat[z]
    top = jnp.max(r.lat_scores[...], axis=0, keepdims=True)
    weight = jnp.exp(r.lat_scores[...] - top)
    total = jnp.sum(weight, axis=0, keepdims=True)
    mixed = jnp.sum(weight * r.lat_gprob[...], axis=0, keepdims=True)
    each(1, NZ, lambda k: stat_to(k).wait_recv())
    best = top
    for i in range(NZ):
        best = jnp.maximum(best, r.stat_got[i, 0])
    total = total * jnp.exp(top - best)
    mixed = mixed * jnp.exp(top - best)
    for i in range(NZ):
        factor = jnp.exp(r.stat_got[i, 0] - best)
        total = total + factor
        mixed = mixed + r.stat_got[i, 1] * factor
    r.stat_own[0] = best + jnp.log(total)
    r.stat_own[1] = mixed / total

    def stat_from(k):
        return push(r.stat_own, r.stat_all.at[z], *sems("stat_from", k), at_z(k)[1])

    each(1, NZ, lambda k: stat_from(k).start())
    r.stat_all[z] = r.stat_own[...]

    prob = jnp.exp(r.lat_scores[...] - r.stat_own[0])
    lat_low = prob.astype(BF16)
    lat_gs = (prob * (r.lat_gprob[...] - r.stat_own[1])).astype(BF16)
    r.lat_out[0] = head_blocks(lat_gs, r.lat_kv[:, :INNER])
    r.lat_out[1] = dot(lat_gs, r.qrow[...])
    r.lat_out[2] = dot(lat_low, r.gorow[z])
    r.lat_out[3] = head_blocks(lat_low, r.lat_kv[:, INNER:])
    each(1, NZ, lambda k: stat_from(k).wait_recv())

    @pl.loop(0, NZ, unroll=4)
    def _(s):
        prob = jnp.exp(r.scores[s] - r.stat_all[s, 0])
        low = prob.astype(BF16)
        r.gs[s] = (prob * (r.gprob[s] - r.stat_all[s, 1])).astype(BF16)
        r.gkv[s, :, INNER:] = dot(low, r.gorow[s]).astype(BF16)
        r.low[s] = low

    gs = r.gs[...].reshape(NZ * KEYS, INNER)
    r.gkv[:, :, :INNER] = dot(gs, r.qrow[...]).astype(BF16).reshape(NZ, KEYS, INNER)
    gkv = r.gkv[...].reshape(NZ * KEYS, 2 * INNER)

    def back_x(k):
        xx, to = at_x(k)
        return push(r.back.at[xx], r.back_got.at[x], *sems("back_x", k), to)

    for i in range(NX):
        span = slice(i * SLOTS, i * SLOTS + SLOTS)
        r.back[i] = dot(r.resorting[span], gkv).astype(BF16)
    for k in (1, 3, 2):
        back_x(k).start()

    def near(d):
        return push(r.part.at[lax.rem(z + NEAR[d], 4)], r.near_in.at[d], *sems("near", d), at_z(NEAR[d])[1])

    def far(i):
        return push(r.far_out.at[lax.rem(lax.div(z, 4) + i, 4)], r.far_in.at[i], *sems("far", i), at_z(4 * i)[1])

    @pl.loop(0, NZ, unroll=4)
    def _(s):
        r.part[s & 3, s >> 2] = head_blocks(r.low[s], r.kvs[s, :, INNER : 2 * INNER]).astype(BF16)

    for d in range(3):
        near(d).start()
    gquery = (head_blocks(gs, r.kvs[:, :, :INNER].reshape(NZ * KEYS, INNER)) + r.lat_out[0]) * HEAD**-0.5
    own = jnp.concatenate([gquery, r.lat_out[1], r.lat_out[2]], axis=1)
    for c in range(2):
        for p in range(NP):
            for j in range(3):
                first = c * 768 + p % 2 * 384 + j * 128
                r.sums[c, p, j] = own[p // 2 * 8 : p // 2 * 8 + 8, first : first + 128]
    sum_core = push(r.sums.at[other], r.sums_core, *sems("sum_core", 0), partner)
    sum_core.start()
    sum_core.wait_recv()

    @pl.loop(0, NP)
    def _(p):
        r.sums_core[p] = r.sums_core[p] + r.sums[core, p]

    def sum_plane(k):
        p, to = at_plane(k)
        return push(r.sums_core.at[p], r.sums_plane.at[me], *sems("sum_plane", k), to)

    each(1, NP, lambda k: sum_plane(k).start())
    r.sums_plane[me] = r.sums_core[me]
    for k in (1, 3, 2):
        back_x(k).wait_recv()
    r.back_got[x] = r.back[x]

    r.kv[:, : 2 * INNER] = dot(r.mine[...], r.back_got[...].reshape(NX * SLOTS, 2 * INNER)).astype(BF16)
    grad_norm = 0.0
    for c in range(2):
        for u in range(2):
            lanes = slice(c * 512 + u * 256, c * 512 + u * 256 + 256)
            grad_norm = grad_norm + dot_nt(r.kv[:, lanes], kv_proj(c, u))
    r.normed[...] = grad_norm.astype(BF16)
    for i in range(4):
        lanes = slice(i * 384, i * 384 + 384)
        natural = dot_nt(r.normed[:, lanes], r.order[...])
        term = jnp.sum(natural * r.hat[:, lanes], axis=0, keepdims=True)
        for j in range(3):
            r.media[i * 3 + j] = term[:, j * 128 : j * 128 + 128]
    med_core = push(r.media, r.media_core, *sems("med_core", 0), partner)
    med_core.start()
    each(1, NP, lambda k: sum_plane(k).wait_recv())
    partial = r.sums_plane[0]
    for p in range(1, NP):
        partial = partial + r.sums_plane[p]
    r.chunk[...] = partial

    def z_far(src, got, name, j):
        return push(src, got.at[lax.div(z, 4)], *sems(name, j), at_z(4 * j)[1])

    def z_near(got, name, d):
        block = got.at[lax.rem(z, 4)]
        return push(block, block, *sems(name, d), at_z(NEAR[d])[1])

    def four(ref):
        return ref[0] + ref[1] + ref[2] + ref[3]

    def sum_far(j):
        return z_far(r.chunk, r.sum_quads, "sum_far", j)

    def sum_near(d):
        return z_near(r.sum_class, "sum_near", d)

    def med_far(j):
        return z_far(r.media_core, r.med_quads, "med_far", j)

    def med_near(d):
        return z_near(r.med_class, "med_near", d)

    for j in (2, 1, 3):
        sum_far(j).start()
    r.sum_quads[lax.div(z, 4)] = r.chunk[...]
    med_core.wait_recv()

    r.media_core[...] = r.media_core[...] + r.media[...]

    for j in (2, 1, 3):
        med_far(j).start()
    r.med_quads[lax.div(z, 4)] = r.media_core[...]
    for j in range(1, 4):
        sum_far(j).wait_recv()
    r.sum_class[lax.rem(z, 4)] = four(r.sum_quads)
    for d in range(3):
        sum_near(d).start()
    for d in range(3):
        near(d).wait_recv()
    for j in range(4):
        value = r.part[lax.rem(z, 4), j].astype(F32)
        for d in range(3):
            value = value + r.near_in[d, j].astype(F32)
        r.far_out[j] = value.astype(BF16)

        @pl.when(lax.div(z, 4) == j)
        def _():
            r.own_part[...] = value

    for i in range(1, 4):
        far(i).start()
    def all_plane(k):
        block = r.whole.at[core, me]
        return push(block, block, *sems("all_plane", k), at_plane(k)[1])

    def all_core(p):
        block = r.whole.at[core, p]
        return push(block, block, *sems("all_core", p), partner)

    def med_all(k):
        block = r.med_whole.at[me]
        return push(block, block, *sems("med_all", k), at_plane(k)[1])

    for j in range(1, 4):
        med_far(j).wait_recv()
    r.med_class[lax.rem(z, 4)] = four(r.med_quads)
    for d in range(3):
        med_near(d).start()
    for d in range(3):
        sum_near(d).wait_recv()
    r.whole[core, me] = four(r.sum_class)
    each(1, NP, lambda k: all_plane(k).start())
    all_core(me).start()
    for d in range(3):
        med_near(d).wait_recv()
    r.med_whole[me] = four(r.med_class)
    each(1, NP, lambda k: med_all(k).start())

    def forward(k):
        all_plane(k).wait_recv()
        all_core(lax.rem(me + NP - k, NP)).start()

    each(1, NP, forward)
    each(0, NP, lambda p: all_core(p).wait_recv())

    def gathered(c, rows, g, j):
        return r.whole[c, rows * 2 + g, j]

    strips = []
    for c in range(2):
        for g in range(2):
            for j in range(3):
                strips.append(jnp.concatenate([gathered(c, rows, g, j) for rows in range(8)], axis=0))

    def precise(values, weight):
        high = values.astype(BF16)
        low = (values - high.astype(F32)).astype(BF16)
        result = dot_nt(jnp.concatenate([high, low], axis=0), weight)
        return result[:LAT] + result[LAT:]

    grad = 0.0
    for i in range(4):
        grad = grad + precise(strips[i], q_proj(i // 2, i % 2))
        both = jnp.concatenate([strips[4 + 2 * i], strips[5 + 2 * i]], axis=1)
        grad = grad + precise(both, kv_proj(i // 2, i % 2))
    natural = []
    for i in range(4):
        rest = grad[:, i * 384 : i * 384 + 384]
        pieces = []
        for _ in range(3):
            high = rest.astype(BF16)
            rest = rest - high.astype(F32)
            pieces.append(high)
        moved = dot_nt(jnp.concatenate(pieces, axis=0), r.order[...])
        natural.append(moved[:LAT] + moved[LAT : 2 * LAT] + moved[2 * LAT :])
    grad = jnp.concatenate(natural, axis=1)
    hat, inverse = norm_rows(r.latents[...])
    r.latent_gain_grad[...] = jnp.sum(grad * hat, axis=0, keepdims=True)
    grad_hat = grad * latent_gain
    r.latent_grad[...] = (
        grad_hat
        - jnp.mean(grad_hat, -1, keepdims=True)
        - hat * jnp.mean(grad_hat * hat, -1, keepdims=True)
    )
    r.lat_inverse[...] = jnp.broadcast_to(inverse, (LAT, 128))
    value = r.own_part[...] + r.lat_out[3]
    for i in range(1, 4):
        far(i).wait_recv()
        value = value + r.far_in[i].astype(F32)
    r.attended[...] = value
    each(1, NP, lambda k: med_all(k).wait_recv())
    value = r.med_whole[0]
    for p in range(1, NP):
        value = value + r.med_whole[p]
    for i in range(12):
        r.media_gain_grad[:, i * 128 : i * 128 + 128] = value[i]

    each(1, NZ, lambda k: along_z(k).wait_send())
    each(1, NZ, lambda k: along_q(k).wait_send())
    for j in range(1, 4):
        go_far(j).wait_send()
        far(j).wait_send()
    for d in range(3):
        near(d).wait_send()
        for i in range(4):
            go_near(i, d).wait_send()
    for ref, name in ((r.wkv, "kv"), (r.wq, "q")):
        for u in range(2):
            for k in range(4):
                if k:
                    second(ref, name + "2", u, k).wait_send()
                    third(ref, name + "3", u, k).wait_send()
                fourth(ref, name + "4", u, k).wait_send()
    for k in range(1, 4):
        out_x(k).wait_send()
        back_x(k).wait_send()
    each(1, NZ, lambda k: stat_to(k).wait_send())
    each(1, NZ, lambda k: stat_from(k).wait_send())
    sum_core.wait_send()
    med_core.wait_send()
    each(1, NP, lambda k: sum_plane(k).wait_send())
    for j in range(1, 4):
        sum_far(j).wait_send()
        med_far(j).wait_send()
    for d in range(3):
        sum_near(d).wait_send()
        med_near(d).wait_send()
    each(1, NP, lambda k: all_plane(k).wait_send())
    each(0, NP, lambda p: all_core(p).wait_send())
    each(1, NP, lambda k: med_all(k).wait_send())


def body(frame_features, frame_owner, latents, latent_gain, media_gain, query_proj, keyval_proj, grad_output):
    route = jnp.repeat(frame_owner[0, :, 0], TOK)
    scratch = [pltpu.VMEM(*spec) for spec in BUFFERS.values()]
    scratch += [DMA(shape) for shape in SEMS.values() for _ in range(2)]
    vmem = pl.BlockSpec(memory_space=pltpu.VMEM)
    attended, latent_grad, lat_inverse, latent_gain_grad, media_gain_grad = pl.pallas_call(
        kernel,
        out_shape=(
            jax.ShapeDtypeStruct((LAT, INNER), F32),
            jax.ShapeDtypeStruct((LAT, WIDTH), F32),
            jax.ShapeDtypeStruct((LAT, 128), F32),
            jax.ShapeDtypeStruct((1, WIDTH), F32),
            jax.ShapeDtypeStruct((1, WIDTH), F32),
        ),
        in_specs=[vmem] * len(INPUTS),
        out_specs=(vmem,) * len(OUTPUTS),
        scratch_shapes=scratch,
        compiler_params=pltpu.CompilerParams(collective_id=0, has_side_effects=True, vmem_limit_bytes=60 << 20),
        name="resampler",
    )(
        keyval_proj,
        query_proj,
        frame_features.reshape(ROWS, WIDTH),
        latents,
        latent_gain,
        media_gain,
        jnp.broadcast_to(route[:, None], (ROWS, 128)),
        grad_output[0, 0],
    )
    latent_grad = latent_grad * lat_inverse[:, :1]
    return (attended.astype(BF16)[None, None], latent_grad, latent_gain_grad[0], media_gain_grad[0])


def solution(mesh):
    placed = (
        P("dp", "frame", None, None),
        P("dp", "frame", None),
        P(),
        P(),
        P(),
        P(("dp", "frame"), None),
        P(("dp", "frame"), None),
        P("dp", "frame", None, None),
    )
    return jax.shard_map(
        body,
        mesh=mesh,
        in_specs=placed,
        out_specs=(P("dp", "frame", None, None), P(), P(), P()),
        check_vma=False,
    )
```

time: 163 us -> 144 us (0.88)
  Pallas kernels: 152 us -> 137 us
  local copies, waits for them, and re-layouts: 8.29 us -> 1.75 us
  other arithmetic: 1.87 us -> 4.63 us
    pallas_call x1, Pallas kernels: 152 us -> 137 us  [body(): pl.pallas_call(kernel, out_shape=(jax.ShapeDtypeStruct((LAT, INNER), F32)...]
    unnamed x14 -> x8, local copies, waits for them, and re-layouts: 4.86 us -> 0.73 us
    mul x0 -> x1, other arithmetic: none -> 1.85 us  [body(): latent_grad = latent_grad * lat_inverse[:, :1]]
where the time goes in v3:
time: 144 us
  Pallas kernels  137 us (95%)
  other arithmetic  4.63 us (3%)
  local copies, waits for them, and re-layouts  1.75 us (1%)
    pallas_call x1, Pallas kernels, body(): pl.pallas_call(kernel, out_shape=(jax.ShapeDtypeStruct((LAT, INNER), F32)...  137 us

profile of v3, /device:TPU:1, one launch (start us, length us, event | category | flops | bytes accessed | tf_op | source)
XLA Modules:
  0.0 143.8 jit_solution(13656284848859972884)
XLA Ops:
  0.6 0.0 copy-start.3
  0.6 0.6 copy-done.3
  1.3 0.1 broadcast_in_dim.13
  1.4 0.1 broadcast_in_dim.14
  1.4 0.8 broadcast_in_dim.15.refs_6_
  2.2 136.8 %resampler.1 = (f32[64,512]{1,0:T(8,128)}, f32[64,1536]{1,0:T(8,128)}, f32[64,128]{1,0:T(8,128)}, f32[1,1536]{1,0:T(1,128)}, f32[1,1536]{1,0:T(1,128)}) custom-call(bf16[3,1024]{1,0:T(4,128)(2,1)} %refs_0_.1, bf16[3,512]{1,0:T(4,128)(2,1)} %refs_1_.1, bf16[256,1536]{1,0:T(8,128)(2,1)} %bitcast.5, f32[64,1536]{1,0:T(8,128)} %refs_3_.1, f32[1536]{0:T(1024)} %refs_4_.1, ...), custom_call_target="tpu_custom_call" | custom-call | tf_op jit(solution)/shard_map/resampler/pallas_call | solution.py:697
  139.0 0.0 copy-start
  139.0 1.5 %convert_bitcast_fusion = bf16[1,1,64,512]{3,2,1,0:T(8,128)(2,1)} fusion(f32[64,512]{1,0:T(8,128)} %get-tuple-element.9), kind=kLoop, calls=%fused_computation.1 | loop fusion | flops 32768 | bytes 196608 | tf_op jit(solution)/shard_map/broadcast_in_dim | solution.py:722
  140.5 0.0 copy-done
  140.5 0.1 slice_reduce_fusion
  140.7 0.0 copy-start.2
  140.7 1.9 %broadcast_multiply_fusion = f32[64,1536]{1,0:T(8,128)} fusion(f32[64,1536]{1,0:T(8,128)} %get-tuple-element.10, f32[64]{0:T(128)S(1)} %slice_reduce_fusion), kind=kLoop, calls=%fused_computation | loop fusion | flops 98304 | bytes 786688 | tf_op jit(solution)/shard_map/mul | solution.py:721
  142.5 0.0 copy-done.2
  142.5 0.0 copy-start.1
  142.5 0.6 reduce.1
  143.1 0.1 copy-done.1
  143.2 0.6 reduce.2
Async XLA Ops:
  0.6 0.7 copy-start.3
  139.0 1.6 %copy-start = (f32[64,128]{1,0:T(8,128)S(1)}, f32[64,128]{1,0:T(8,128)}, u32[]{:S(2)}) copy-start(f32[64,128]{1,0:T(8,128)} %get-tuple-element.11) | copy-start | bytes 98308
  140.7 1.9 %copy-start.2 = (f32[1,1536]{1,0:T(1,128)S(1)}, f32[1,1536]{1,0:T(1,128)}, u32[]{:S(2)}) copy-start(f32[1,1536]{1,0:T(1,128)} %get-tuple-element.12) | copy-start | bytes 18436
  142.5 0.7 copy-start.1

commit v4 on v3

--- a/solution.py
+++ b/solution.py
@@ -113,6 +113,7 @@
     got=((NX, SLOTS, SEND), BF16),
     kvs=((NZ, KEYS, SEND), BF16),
     lat_normed=((LAT, WIDTH), BF16),
+    lat_hat=((LAT, WIDTH), F32),
     lat_kv=((LAT, 2 * INNER), BF16),
     qrow=((HEADS * LAT, INNER), BF16),
     gorow=((NZ, HEADS * LAT, INNER), BF16),
@@ -198,12 +199,17 @@
         def _(k):
             act(k)
 
+    def far_first(act):
+        @pl.loop(0, NZ - 1)
+        def _(i):
+            act(NZ // 2 + ((i + 1) >> 1) * (1 - 2 * (i & 1)))
+
     barrier = pltpu.get_barrier_semaphore()
 
     def greet(to):
         pl.semaphore_signal(barrier, inc=1, device_id=to, device_id_type=MESH)
 
-    each(1, NZ, lambda k: greet(at_z(k)[1]))
+    far_first(lambda k: greet(at_z(k)[1]))
     each(1, NP, lambda k: greet(at_plane(k)[1]))
     greet(partner)
     r.gob[z] = r.grad[...]
@@ -238,7 +244,9 @@
         r.gorow[s] = jnp.zeros((HEADS * LAT, INNER), BF16)
 
     reorder(r.normed)
-    hat, _ = norm_rows(r.latents[...])
+    hat, inverse = norm_rows(r.latents[...])
+    r.lat_hat[...] = hat
+    r.lat_inverse[...] = jnp.broadcast_to(inverse, (LAT, 128))
     r.lat_normed[...] = (hat * latent_gain).astype(BF16)
     reorder(r.lat_normed)
     def slot_owner(slot):
@@ -274,8 +282,8 @@
     def along_q(k):
         return push(r.zq.at[z], r.zq.at[z], *sems("along_q", k), at_z(k)[1])
 
-    each(1, NZ, lambda k: along_z(k).start())
-    each(1, NZ, lambda k: along_q(k).start())
+    far_first(lambda k: along_z(k).start())
+    far_first(lambda k: along_q(k).start())
     each(1, NZ, lambda k: along_z(k).wait_recv())
     for k in range(NZ):
         r.rows[6 * k : 6 * k + 6, :512] = r.zkv[k, 0:6].astype(F32)
@@ -403,12 +411,27 @@
         zz, to = at_z(k)
         return push(r.stat.at[zz], r.stat_got.at[z], *sems("stat_to", k), to)
 
-    each(1, NZ, lambda k: stat_to(k).start())
+    far_first(lambda k: stat_to(k).start())
     r.stat_got[z] = r.stat[z]
     top = jnp.max(r.lat_scores[...], axis=0, keepdims=True)
     weight = jnp.exp(r.lat_scores[...] - top)
     total = jnp.sum(weight, axis=0, keepdims=True)
     mixed = jnp.sum(weight * r.lat_gprob[...], axis=0, keepdims=True)
+    each(1, NZ, lambda k: along_z(k).wait_send())
+    each(1, NZ, lambda k: along_q(k).wait_send())
+    for j in range(1, 4):
+        go_far(j).wait_send()
+        out_x(j).wait_send()
+    for d in range(3):
+        for i in range(4):
+            go_near(i, d).wait_send()
+    for ref, name in ((r.wkv, "kv"), (r.wq, "q")):
+        for u in range(2):
+            for k in range(4):
+                if k:
+                    second(ref, name + "2", u, k).wait_send()
+                    third(ref, name + "3", u, k).wait_send()
+                fourth(ref, name + "4", u, k).wait_send()
     each(1, NZ, lambda k: stat_to(k).wait_recv())
     best = top
     for i in range(NZ):
@@ -425,7 +448,7 @@
     def stat_from(k):
         return push(r.stat_own, r.stat_all.at[z], *sems("stat_from", k), at_z(k)[1])
 
-    each(1, NZ, lambda k: stat_from(k).start())
+    far_first(lambda k: stat_from(k).start())
     r.stat_all[z] = r.stat_own[...]
 
     prob = jnp.exp(r.lat_scores[...] - r.stat_own[0])
@@ -549,11 +572,6 @@
     for j in (2, 1, 3):
         med_far(j).start()
     r.med_quads[lax.div(z, 4)] = r.media_core[...]
-    for j in range(1, 4):
-        sum_far(j).wait_recv()
-    r.sum_class[lax.rem(z, 4)] = four(r.sum_quads)
-    for d in range(3):
-        sum_near(d).start()
     for d in range(3):
         near(d).wait_recv()
     for j in range(4):
@@ -568,6 +586,11 @@
 
     for i in range(1, 4):
         far(i).start()
+    for j in range(1, 4):
+        sum_far(j).wait_recv()
+    r.sum_class[lax.rem(z, 4)] = four(r.sum_quads)
+    for d in range(3):
+        sum_near(d).start()
     def all_plane(k):
         block = r.whole.at[core, me]
         return push(block, block, *sems("all_plane", k), at_plane(k)[1])
@@ -594,6 +617,15 @@
         med_near(d).wait_recv()
     r.med_whole[me] = four(r.med_class)
     each(1, NP, lambda k: med_all(k).start())
+
+    each(1, NZ, lambda k: stat_to(k).wait_send())
+    for k in range(1, 4):
+        back_x(k).wait_send()
+    for d in range(3):
+        near(d).wait_send()
+    sum_core.wait_send()
+    med_core.wait_send()
+    each(1, NP, lambda k: sum_plane(k).wait_send())
 
     def forward(k):
         all_plane(k).wait_recv()
@@ -633,7 +665,7 @@
         moved = dot_nt(jnp.concatenate(pieces, axis=0), r.order[...])
         natural.append(moved[:LAT] + moved[LAT : 2 * LAT] + moved[2 * LAT :])
     grad = jnp.concatenate(natural, axis=1)
-    hat, inverse = norm_rows(r.latents[...])
+    hat = r.lat_hat[...]
     r.latent_gain_grad[...] = jnp.sum(grad * hat, axis=0, keepdims=True)
     grad_hat = grad * latent_gain
     r.latent_grad[...] = (
@@ -641,7 +673,6 @@
         - jnp.mean(grad_hat, -1, keepdims=True)
         - hat * jnp.mean(grad_hat * hat, -1, keepdims=True)
     )
-    r.lat_inverse[...] = jnp.broadcast_to(inverse, (LAT, 128))
     value = r.own_part[...] + r.lat_out[3]
     for i in range(1, 4):
         far(i).wait_recv()
@@ -653,32 +684,9 @@
         value = value + r.med_whole[p]
     for i in range(12):
         r.media_gain_grad[:, i * 128 : i * 128 + 128] = value[i]
-
-    each(1, NZ, lambda k: along_z(k).wait_send())
-    each(1, NZ, lambda k: along_q(k).wait_send())
+    each(1, NZ, lambda k: stat_from(k).wait_send())
     for j in range(1, 4):
-        go_far(j).wait_send()
         far(j).wait_send()
-    for d in range(3):
-        near(d).wait_send()
-        for i in range(4):
-            go_near(i, d).wait_send()
-    for ref, name in ((r.wkv, "kv"), (r.wq, "q")):
-        for u in range(2):
-            for k in range(4):
-                if k:
-                    second(ref, name + "2", u, k).wait_send()
-                    third(ref, name + "3", u, k).wait_send()
-                fourth(ref, name + "4", u, k).wait_send()
-    for k in range(1, 4):
-        out_x(k).wait_send()
-        back_x(k).wait_send()
-    each(1, NZ, lambda k: stat_to(k).wait_send())
-    each(1, NZ, lambda k: stat_from(k).wait_send())
-    sum_core.wait_send()
-    med_core.wait_send()
-    each(1, NP, lambda k: sum_plane(k).wait_send())
-    for j in range(1, 4):
         sum_far(j).wait_send()
         med_far(j).wait_send()
     for d in range(3):

time: 144 us -> 140 us (0.972)
  Pallas kernels: 137 us -> 132 us
    pallas_call x1, Pallas kernels: 137 us -> 132 us  [body(): pl.pallas_call(kernel, out_shape=(jax.ShapeDtypeStruct((LAT, INNER), F32)...]
where the time goes in v4:
time: 140 us; the launch traced here: 139 us
  Pallas kernels  132 us (94%)
  other arithmetic  4.63 us (3%)
  local copies, waits for them, and re-layouts  1.75 us (1%)
    pallas_call x1, Pallas kernels, body(): pl.pallas_call(kernel, out_shape=(jax.ShapeDtypeStruct((LAT, INNER), F32)...  132 us

profile of v4, /device:TPU:1, one launch (start us, length us, event | category | flops | bytes accessed | tf_op | source)
XLA Modules:
  0.0 139.4 jit_solution(7415065074631185117)
XLA Ops:
  0.6 0.0 copy-start.3
  0.6 0.6 copy-done.3
  1.3 0.1 broadcast_in_dim.13
  1.4 0.1 broadcast_in_dim.14
  1.4 0.8 broadcast_in_dim.15.refs_6_
  2.2 132.4 %resampler.1 = (f32[64,512]{1,0:T(8,128)}, f32[64,1536]{1,0:T(8,128)}, f32[64,128]{1,0:T(8,128)}, f32[1,1536]{1,0:T(1,128)}, f32[1,1536]{1,0:T(1,128)}) custom-call(bf16[3,1024]{1,0:T(4,128)(2,1)} %refs_0_.1, bf16[3,512]{1,0:T(4,128)(2,1)} %refs_1_.1, bf16[256,1536]{1,0:T(8,128)(2,1)} %bitcast.5, f32[64,1536]{1,0:T(8,128)} %refs_3_.1, f32[1536]{0:T(1024)} %refs_4_.1, ...), custom_call_target="tpu_custom_call" | custom-call | tf_op jit(solution)/shard_map/resampler/pallas_call | solution.py:705
  134.6 0.0 copy-start
  134.6 1.5 %convert_bitcast_fusion = bf16[1,1,64,512]{3,2,1,0:T(8,128)(2,1)} fusion(f32[64,512]{1,0:T(8,128)} %get-tuple-element.9), kind=kLoop, calls=%fused_computation.1 | loop fusion | flops 32768 | bytes 196608 | tf_op jit(solution)/shard_map/broadcast_in_dim | solution.py:730
  136.1 0.0 copy-done
  136.1 0.1 slice_reduce_fusion
  136.3 0.0 copy-start.2
  136.3 1.9 %broadcast_multiply_fusion = f32[64,1536]{1,0:T(8,128)} fusion(f32[64,1536]{1,0:T(8,128)} %get-tuple-element.10, f32[64]{0:T(128)S(1)} %slice_reduce_fusion), kind=kLoop, calls=%fused_computation | loop fusion | flops 98304 | bytes 786688 | tf_op jit(solution)/shard_map/mul | solution.py:729
  138.1 0.0 copy-done.2
  138.1 0.0 copy-start.1
  138.1 0.6 reduce.1
  138.7 0.1 copy-done.1
  138.8 0.6 reduce.2
Async XLA Ops:
  0.6 0.7 copy-start.3
  134.6 1.6 %copy-start = (f32[64,128]{1,0:T(8,128)S(1)}, f32[64,128]{1,0:T(8,128)}, u32[]{:S(2)}) copy-start(f32[64,128]{1,0:T(8,128)} %get-tuple-element.11) | copy-start | bytes 98308
  136.3 1.9 %copy-start.2 = (f32[1,1536]{1,0:T(1,128)S(1)}, f32[1,1536]{1,0:T(1,128)}, u32[]{:S(2)}) copy-start(f32[1,1536]{1,0:T(1,128)} %get-tuple-element.12) | copy-start | bytes 18436
  138.1 0.7 copy-start.1
